TPU v7x, 128 devices: a whole 4x4x4 slice. The times are simulated.
128 devices in a mesh: sx: 16 (over y_hi, x, core), sy: 8 (over z, y_lo).
Axes of the slice: x: 4, y: 4 (y_hi: 2, y_lo: 2; y = y_hi * 2 + y_lo), z: 4, core: 2. Of those that a mesh axis runs over, the one named last changes fastest.
Arguments:
- weights: bfloat16 [2048, 1024, 128], P('sx', 'sy'), may hold values from -6 to 6
- velocity: bfloat16 [2048, 1024], P('sx', 'sy'), may hold values from 0.5 to 3
- translation: bfloat16 [2, 2, 2, 2, 64, 64], replicated, may hold values from -0.375 to 0.375
Outputs:
- final_weights: float32 [2048, 1024, 128], P('sx', 'sy')
All inputs are finite; a program needn't handle non-finite values.
Results may differ from a plain program's by a relative error of at most 0.0081.
Values may be sent and summed in bfloat16 or wider, within the bound.
No kernel may reach another device: no remote copies, remote signals or barrier semaphores. Data moves between devices by JAX's collectives and lax.ppermute only.
A program may use at most 128 MiB of HBM per device.

v0:
```python
import jax
import jax.numpy as jnp
from jax import lax
from jax.sharding import PartitionSpec as P

LEVELS = 8


def from_partner(x, axis, stride):
    return lax.ppermute(x, axis, [(i, i ^ 1 << stride) for i in range(lax.axis_size(axis))])


def node_totals():
    counter = jnp.arange(8, dtype=jnp.float32)
    nodes = jnp.cos(jnp.pi * (2.0 * counter + 1.0) / 16.0)
    return (nodes[:, None] + nodes[None, :]).reshape(64)


def phase_angles(velocity, level_index):
    totals = node_totals()
    return velocity.astype(jnp.float32)[..., None] * totals * (0.5 * (level_index + 1))


def rotate_phase(values, angles, sign):
    cosine = jnp.cos(angles)
    sine = sign * jnp.sin(angles)
    real_part = values[..., :64]
    imag_part = values[..., 64:]
    return jnp.concatenate(
        [real_part * cosine - imag_part * sine, real_part * sine + imag_part * cosine], axis=-1
    )


def block_matrices(translation, dim_index):
    blocks = translation[dim_index]
    upper = jnp.concatenate([blocks[:, :, 0], blocks[:, :, 1]], axis=-1)
    lower = jnp.concatenate([-blocks[:, :, 1], blocks[:, :, 0]], axis=-1)
    return jnp.concatenate([upper, lower], axis=-2)


def combine_pairs(first, second, matrices):
    outputs = []
    for target in range(2):
        term = jnp.dot(first, matrices[target, 0], preferred_element_type=jnp.float32)
        outputs.append(
            term + jnp.dot(second, matrices[target, 1], preferred_element_type=jnp.float32)
        )
    return outputs


def pair_local(mixed, matrices, distance):
    extent_x, extent_y, width = mixed.shape
    grouped = mixed.reshape(extent_x, extent_y // (2 * distance), 2, distance, width)
    outputs = combine_pairs(grouped[:, :, 0], grouped[:, :, 1], matrices)
    return jnp.stack(outputs, axis=2).reshape(extent_x, extent_y, width)


def pair_remote(mixed, partner, matrices, own_bit):
    lower_side = own_bit == 0
    own_matrix = jnp.where(lower_side, matrices[0, 0], matrices[1, 1])
    other_matrix = jnp.where(lower_side, matrices[0, 1], matrices[1, 0])
    own_term = jnp.dot(mixed, own_matrix, preferred_element_type=jnp.float32)
    return own_term + jnp.dot(partner, other_matrix, preferred_element_type=jnp.float32)


def swap_columns(values, bit_index):
    return from_partner(values, "sx", bit_index)


def swap_rows(values, bit_index):
    return from_partner(values, "sy", bit_index)


def bit_of(ratio):
    return ratio.bit_length() - 1


def shards(weights, velocity, translation):
    rows_x, rows_y = velocity.shape
    count_x = lax.axis_size("sx")
    count_y = lax.axis_size("sy")
    total_x = rows_x * count_x
    total_y = rows_y * count_y
    start_x = lax.axis_index("sx") * rows_x
    start_y = lax.axis_index("sy") * rows_y
    state = weights.astype(jnp.float32)
    for level_index in range(LEVELS):
        dim_index = level_index % 2
        depth = level_index // 2
        angles = phase_angles(velocity, level_index)
        mixed = rotate_phase(state, angles, -1.0).astype(jnp.bfloat16)
        matrices = block_matrices(translation, dim_index)
        if dim_index == 0:
            distance = total_x >> depth + 1
            extent = state.shape[0]
            start = start_x
        else:
            distance = total_y >> depth + 1
            extent = state.shape[1]
            start = start_y
        if distance < extent:
            joined = pair_local(mixed, matrices, distance)
        else:
            if dim_index == 0:
                partner = swap_columns(mixed, bit_of(distance // extent))
            else:
                partner = swap_rows(mixed, bit_of(distance // rows_y))
            own_bit = start // distance % 2
            joined = pair_remote(mixed, partner, matrices, own_bit)
        state = rotate_phase(joined, angles, 1.0)
    return state


def solution(mesh):
    placed = (P("sx", "sy", None), P("sx", "sy"), P())
    return jax.shard_map(
        shards, mesh=mesh, in_specs=placed, out_specs=P("sx", "sy", None), check_vma=False
    )
```

profile of v0, /device:TPU:1, one launch (start us, length us, event | category | flops | bytes accessed | tf_op | source)
XLA Modules:
  0.0 921.7 jit_solution(9539283472782255601)
XLA Ops:
  0.2 0.8 convert_element_type.12
  1.0 6.4 copy.60
  7.3 3.3 convert_element_type.11
  10.6 16.5 %fusion.87 = (bf16[128,128,64]{1,2,0:T(8,128)(2,1)S(1)}, bf16[128,128,64]{1,2,0:T(8,128)(2,1)S(1)}) fusion(f32[128,128,128]{1,2,0:T(8,128)S(1)} %convert_element_type.11, f32[64]{0:T(128)S(1)} %add.197, f32[128,128]{1,0:T(8,128)S(1)} %convert_element_type.12), kind=kLoop, calls=%fused_computation.98 | loop fusion | flops 11534336 | bytes 12648704 | tf_op jit(solution)/shard_map/convert.16
  27.1 2.7 pad_maximum_fusion.2
  29.8 3.7 collective-permute-start
  33.6 0.1 maximum_maximum_fusion.1
  33.8 2.9 fusion.153
  36.6 87.3 %collective-permute-done = bf16[128,128,128]{1,2,0:T(8,128)(2,1)} collective-permute-done((bf16[128,128,128]{1,2,0:T(8,128)(2,1)}, bf16[128,128,128]{1,2,0:T(8,128)(2,1)}, u32[]{:S(2)}, u32[]{:S(2)}) %collective-permute-start) | collective-permute-done | bytes 4194336 | tf_op jit(solution)/shard_map/ppermute | solution.py:10
  123.9 3.5 convolution_add_fusion.6
  127.4 31.6 %fusion.115 = (bf16[128,128,64]{1,2,0:T(8,128)(2,1)S(1)}, bf16[128,128,64]{1,2,0:T(8,128)(2,1)S(1)}) fusion(f32[64]{0:T(128)S(1)} %add.197, f32[128,128]{1,0:T(8,128)S(1)} %convert_element_type.12, f32[128,128,128]{1,2,0:T(8,128)S(1)} %convolution_add_fusion.6), kind=kLoop, calls=%fused_computation.126 | loop fusion | flops 17825792 | bytes 12648704 | tf_op jit(solution)/shard_map/convert.14
  159.0 2.7 pad_maximum_fusion.3
  161.7 3.8 collective-permute-start.1
  165.5 0.1 copy.127
  165.7 0.1 maximum_maximum_fusion
  165.8 2.8 fusion.165
  168.7 86.5 %collective-permute-done.1 = bf16[128,128,128]{1,2,0:T(8,128)(2,1)} collective-permute-done((bf16[128,128,128]{1,2,0:T(8,128)(2,1)}, bf16[128,128,128]{1,2,0:T(8,128)(2,1)}, u32[]{:S(2)}, u32[]{:S(2)}) %collective-permute-start.1) | collective-permute-done | bytes 4194336 | tf_op jit(solution)/shard_map/ppermute | solution.py:10
  255.2 3.4 convolution_add_fusion.2
  258.6 31.6 %fusion.91 = (bf16[128,128,64]{1,2,0:T(8,128)(2,1)S(1)}, bf16[128,128,64]{1,2,0:T(8,128)(2,1)S(1)}) fusion(f32[64]{0:T(128)S(1)} %add.197, f32[128,128]{1,0:T(8,128)S(1)} %convert_element_type.12, f32[128,128,128]{1,2,0:T(8,128)S(1)} %convolution_add_fusion.2), kind=kLoop, calls=%fused_computation.102 | loop fusion | flops 17825792 | bytes 12648704 | tf_op jit(solution)/shard_map/convert.12
  290.3 2.7 pad_maximum_fusion.4
  293.0 3.0 collective-permute-start.2
  296.0 2.9 fusion.150
  298.9 86.1 %collective-permute-done.2 = bf16[128,128,128]{1,2,0:T(8,128)(2,1)} collective-permute-done((bf16[128,128,128]{1,2,0:T(8,128)(2,1)}, bf16[128,128,128]{1,2,0:T(8,128)(2,1)}, u32[]{:S(2)}, u32[]{:S(2)}) %collective-permute-start.2) | collective-permute-done | bytes 4194336 | tf_op jit(solution)/shard_map/ppermute | solution.py:10
  384.9 3.5 convolution_add_fusion.5
  388.4 31.8 %fusion.95 = (bf16[128,128,64]{1,2,0:T(8,128)(2,1)S(1)}, bf16[128,128,64]{1,2,0:T(8,128)(2,1)S(1)}) fusion(f32[64]{0:T(128)S(1)} %add.197, f32[128,128]{1,0:T(8,128)S(1)} %convert_element_type.12, f32[128,128,128]{1,2,0:T(8,128)S(1)} %convolution_add_fusion.5), kind=kLoop, calls=%fused_computation.106 | loop fusion | flops 18874368 | bytes 12648704 | tf_op jit(solution)/shard_map/convert.10
  420.2 2.7 pad_maximum_fusion.5
  422.9 0.9 collective-permute-start.3
  423.8 2.8 fusion.159
  426.6 86.0 %collective-permute-done.3 = bf16[128,128,128]{1,2,0:T(8,128)(2,1)} collective-permute-done((bf16[128,128,128]{1,2,0:T(8,128)(2,1)}, bf16[128,128,128]{1,2,0:T(8,128)(2,1)}, u32[]{:S(2)}, u32[]{:S(2)}) %collective-permute-start.3) | collective-permute-done | bytes 4194336 | tf_op jit(solution)/shard_map/ppermute | solution.py:10
  512.6 3.4 convolution_add_fusion.1
  516.1 31.8 %fusion.99 = (bf16[128,128,64]{1,2,0:T(8,128)(2,1)S(1)}, bf16[128,128,64]{1,2,0:T(8,128)(2,1)S(1)}) fusion(f32[64]{0:T(128)S(1)} %add.197, f32[128,128]{1,0:T(8,128)S(1)} %convert_element_type.12, f32[128,128,128]{1,2,0:T(8,128)S(1)} %convolution_add_fusion.1), kind=kLoop, calls=%fused_computation.110 | loop fusion | flops 18874368 | bytes 12648704 | tf_op jit(solution)/shard_map/convert.8
  547.9 2.7 pad_maximum_fusion.6
  550.6 1.4 collective-permute-start.4
  551.9 2.9 fusion.147
  554.8 84.3 %collective-permute-done.4 = bf16[128,128,128]{1,2,0:T(8,128)(2,1)} collective-permute-done((bf16[128,128,128]{1,2,0:T(8,128)(2,1)}, bf16[128,128,128]{1,2,0:T(8,128)(2,1)}, u32[]{:S(2)}, u32[]{:S(2)}) %collective-permute-start.4) | collective-permute-done | bytes 4194336 | tf_op jit(solution)/shard_map/ppermute | solution.py:10
  639.1 3.5 convolution_add_fusion.4
  642.6 31.8 %fusion.103 = (bf16[128,128,64]{1,2,0:T(8,128)(2,1)S(1)}, bf16[128,128,64]{1,2,0:T(8,128)(2,1)S(1)}) fusion(f32[64]{0:T(128)S(1)} %add.197, f32[128,128]{1,0:T(8,128)S(1)} %convert_element_type.12, f32[128,128,128]{1,2,0:T(8,128)S(1)} %convolution_add_fusion.4), kind=kLoop, calls=%fused_computation.114 | loop fusion | flops 18874368 | bytes 12648704 | tf_op jit(solution)/shard_map/convert.6
  674.4 2.7 pad_maximum_fusion.7
  677.1 1.5 collective-permute-start.5
  678.5 2.8 fusion.156
  681.4 83.3 %collective-permute-done.5 = bf16[128,128,128]{1,2,0:T(8,128)(2,1)} collective-permute-done((bf16[128,128,128]{1,2,0:T(8,128)(2,1)}, bf16[128,128,128]{1,2,0:T(8,128)(2,1)}, u32[]{:S(2)}, u32[]{:S(2)}) %collective-permute-start.5) | collective-permute-done | bytes 4194336 | tf_op jit(solution)/shard_map/ppermute | solution.py:10
  764.7 3.4 convolution_add_fusion
  768.1 31.8 %fusion.107 = (bf16[128,128,64]{1,2,0:T(8,128)(2,1)S(1)}, bf16[128,128,64]{1,2,0:T(8,128)(2,1)S(1)}) fusion(f32[64]{0:T(128)S(1)} %add.197, f32[128,128]{1,0:T(8,128)S(1)} %convert_element_type.12, f32[128,128,128]{1,2,0:T(8,128)S(1)} %convolution_add_fusion), kind=kLoop, calls=%fused_computation.118 | loop fusion | flops 18874368 | bytes 12648704 | tf_op jit(solution)/shard_map/convert.4
  799.9 2.7 pad_maximum_fusion.8
  802.6 6.1 collective-permute-start.6
  808.7 2.9 fusion.144
  811.6 4.2 collective-permute-done.6
  815.9 3.5 convolution_add_fusion.3
  819.3 32.5 %fusion.113 = (bf16[128,128,64]{1,2,0:T(8,128)(2,1)}, bf16[128,128,64]{1,2,0:T(8,128)(2,1)S(1)}) fusion(f32[64]{0:T(128)S(1)} %add.197, f32[128,128]{1,0:T(8,128)S(1)} %convert_element_type.12, f32[128,128,128]{1,2,0:T(8,128)S(1)} %convolution_add_fusion.3), kind=kLoop, calls=%fused_computation.124 | loop fusion | flops 18874368 | bytes 12648704 | tf_op jit(solution)/shard_map/convert.2
  851.8 7.4 copy.124
  859.2 6.7 copy.123
  865.9 3.5 fusion.136
  869.5 1.2 copy-done.1
  870.6 1.3 fusion.138
  871.9 1.3 fusion.141
  873.2 0.7 add_bitcast_fusion.1
  874.0 0.8 add_bitcast_fusion
  874.7 1.1 pad_maximum_fusion
  875.8 4.2 fusion.228
  880.0 5.5 copy.130
  885.5 5.4 copy.129
  890.9 17.4 %fusion.118 = (f32[128,128,64]{1,2,0:T(8,128)S(1)}, f32[128,128,64]{1,2,0:T(8,128)S(1)}) fusion(f32[128,128,64]{1,2,0:T(8,128)} %copy.130, f32[128,128,64]{1,2,0:T(8,128)} %copy.129, f32[64]{0:T(128)S(1)} %add.197, f32[128,128]{1,0:T(8,128)S(1)} %convert_element_type.12), kind=kLoop, calls=%fused_computation.129 | loop fusion | flops 8388608 | bytes 16843008 | tf_op jit(solution)/shard_map/sub | solution.py:30
  908.3 3.9 pad_maximum_fusion.1
  912.2 9.0 copy.92
  (27 shorter events, 0.3 us)
Async XLA Ops:
  27.1 2.7 copy-start.2
  27.1 6.4 copy-start.9
  29.8 94.1 %collective-permute-start = (bf16[128,128,128]{1,2,0:T(8,128)(2,1)}, bf16[128,128,128]{1,2,0:T(8,128)(2,1)}, u32[]{:S(2)}, u32[]{:S(2)}) collective-permute-start(bf16[128,128,128]{1,2,0:T(8,128)(2,1)} %pad_maximum_fusion.2), channel_id=1, source_target_pairs={{0,64},{8,72},{16,80},{24,88},{32,96},{40,104},{48,112},{56,120},{... | collective-permute-start | bytes 12582920 | tf_op jit(solution)/shard_map/ppermute | solution.py:10
  159.0 2.7 copy-start.3
  161.7 93.5 %collective-permute-start.1 = (bf16[128,128,128]{1,2,0:T(8,128)(2,1)}, bf16[128,128,128]{1,2,0:T(8,128)(2,1)}, u32[]{:S(2)}, u32[]{:S(2)}) collective-permute-start(bf16[128,128,128]{1,2,0:T(8,128)(2,1)} %pad_maximum_fusion.3), channel_id=1, source_target_pairs={{0,4},{1,5},{2,6},{3,7},{4,0},{5,1},{6,2},{7,3},{8,12},{9,13},{10,... | collective-permute-start | bytes 12582920 | tf_op jit(solution)/shard_map/ppermute | solution.py:10
  290.3 2.7 copy-start.6
  293.0 91.9 %collective-permute-start.2 = (bf16[128,128,128]{1,2,0:T(8,128)(2,1)}, bf16[128,128,128]{1,2,0:T(8,128)(2,1)}, u32[]{:S(2)}, u32[]{:S(2)}) collective-permute-start(bf16[128,128,128]{1,2,0:T(8,128)(2,1)} %pad_maximum_fusion.4), channel_id=1, source_target_pairs={{0,32},{8,40},{16,48},{24,56},{32,0},{40,8},{48,16},{56,24},{64,96... | collective-permute-start | bytes 12582920 | tf_op jit(solution)/shard_map/ppermute | solution.py:10
  420.2 2.7 copy-start.8
  422.9 89.7 %collective-permute-start.3 = (bf16[128,128,128]{1,2,0:T(8,128)(2,1)}, bf16[128,128,128]{1,2,0:T(8,128)(2,1)}, u32[]{:S(2)}, u32[]{:S(2)}) collective-permute-start(bf16[128,128,128]{1,2,0:T(8,128)(2,1)} %pad_maximum_fusion.5), channel_id=1, source_target_pairs={{0,2},{1,3},{2,0},{3,1},{4,6},{5,7},{6,4},{7,5},{8,10},{9,11},{10,... | collective-permute-start | bytes 12582920 | tf_op jit(solution)/shard_map/ppermute | solution.py:10
  547.9 2.7 copy-start.7
  550.6 88.5 %collective-permute-start.4 = (bf16[128,128,128]{1,2,0:T(8,128)(2,1)}, bf16[128,128,128]{1,2,0:T(8,128)(2,1)}, u32[]{:S(2)}, u32[]{:S(2)}) collective-permute-start(bf16[128,128,128]{1,2,0:T(8,128)(2,1)} %pad_maximum_fusion.6), channel_id=1, source_target_pairs={{0,16},{8,24},{16,0},{24,8},{32,48},{40,56},{48,32},{56,40},{64,80... | collective-permute-start | bytes 12582920 | tf_op jit(solution)/shard_map/ppermute | solution.py:10
  674.4 2.7 copy-start.5
  677.1 87.6 %collective-permute-start.5 = (bf16[128,128,128]{1,2,0:T(8,128)(2,1)}, bf16[128,128,128]{1,2,0:T(8,128)(2,1)}, u32[]{:S(2)}, u32[]{:S(2)}) collective-permute-start(bf16[128,128,128]{1,2,0:T(8,128)(2,1)} %pad_maximum_fusion.7), channel_id=1, source_target_pairs={{0,1},{1,0},{2,3},{3,2},{4,5},{5,4},{6,7},{7,6},{8,9},{9,8},{10,11... | collective-permute-start | bytes 12582920 | tf_op jit(solution)/shard_map/ppermute | solution.py:10
  799.9 2.7 copy-start.4
  802.6 13.2 %collective-permute-start.6 = (bf16[128,128,128]{1,2,0:T(8,128)(2,1)}, bf16[128,128,128]{1,2,0:T(8,128)(2,1)}, u32[]{:S(2)}, u32[]{:S(2)}) collective-permute-start(bf16[128,128,128]{1,2,0:T(8,128)(2,1)} %pad_maximum_fusion.8), channel_id=1, source_target_pairs={{0,8},{8,0},{16,24},{24,16},{32,40},{40,32},{48,56},{56,48},{64,72... | collective-permute-start | bytes 12582920 | tf_op jit(solution)/shard_map/ppermute | solution.py:10
  865.9 3.6 copy-start
  865.9 4.7 copy-start.1
where the time goes:
time: 931 us; the launch traced here: 922 us
  waiting for transfers between devices  518 us (56%)
  other arithmetic  289 us (31%)
  matrix products  48.3 us (5%)
  local copies, waits for them, and re-layouts  45.9 us (5%)
  starting transfers between devices  20.4 us (2%)
    ppermute x7, waiting for transfers between devices, from_partner(): lax.ppermute(x, axis, [(i, i ^ 1 << stride) for i in range(lax.axis_size(...  518 us
    another operation x9, other arithmetic  243 us
    dot_general x7, matrix products, pair_remote(): jnp.dot(partner, other_matrix, preferred_element_type=jnp.float32)  24.2 us
    concatenate x3, local copies, waits for them, and re-layouts, rotate_phase(): jnp.concatenate([real_part * cosine - imag_part * sine, real_part * sine...  23.1 us
    concatenate x8, other arithmetic, rotate_phase(): jnp.concatenate([real_part * cosine - imag_part * sine, real_part * sine...  22.7 us
    ppermute x7, starting transfers between devices, from_partner(): lax.ppermute(x, axis, [(i, i ^ 1 << stride) for i in range(lax.axis_size(...  20.4 us
    dot_general x7, matrix products, pair_remote(): own_term = jnp.dot(mixed, own_matrix, preferred_element_type=jnp.float32)  20 us
  transfers between devices with their start and end apart: 7, of which 7 were waited for; matrix products, arithmetic and copies ran while one was open for 2% of the time, Pallas kernels for 0%

commit v1 on v0

v1 whole, which is shorter than its diff:
```python
import functools

import jax
import jax.numpy as jnp
import numpy as np
from jax import lax
from jax.experimental import pallas as pl
from jax.experimental.pallas import tpu as pltpu
from jax.sharding import PartitionSpec as P

CHUNKS = 2
TERMS = 7
MAX_ANGLE = 2.95
EVERY = ("sx", "sy")


def level_bits(count_x, count_y):
    bits_x = count_x.bit_length() - 1
    bits_y = count_y.bit_length() - 1
    order = []
    for step in range(4):
        order.append(bits_y + bits_x - 1 - step)
        order.append(bits_y - 1 - step if step < bits_y else None)
    return order


def half_totals():
    counter = np.arange(8, dtype=np.float64)
    nodes = np.cos(np.pi * (2.0 * counter + 1.0) / 16.0)
    totals = (nodes[:, None] + nodes[None, :]).reshape(64) * 0.5
    return np.concatenate([totals, totals])


def trig_constants():
    top = MAX_ANGLE**2
    count = 400
    square = (np.cos(np.pi * (np.arange(count) + 0.5) / count) + 1) / 2 * top
    angle = np.sqrt(square)

    def fit(values):
        series = np.polynomial.chebyshev.Chebyshev.fit(square, values, TERMS - 1, domain=[0, top])
        return series.convert(kind=np.polynomial.Polynomial, domain=[-1, 1], window=[-1, 1]).coef

    rows = np.zeros((TERMS + 1, 128), np.float32)
    rows[:TERMS, :64] = fit(np.cos(angle))[:, None]
    rows[:TERMS, 64:] = fit(np.sin(angle) / angle)[:, None]
    rows[TERMS] = half_totals()
    return rows


def swap_parts(values):
    return pltpu.roll(values, 64, values.ndim - 1)


def trig_kernel(const_ref, velocity_ref, trig_ref, *, group):
    sources, half, _ = trig_ref.shape[0], trig_ref.shape[2], 0
    rows = 2 * half
    low_row = pl.program_id(0) * half
    lane = lax.broadcasted_iota(jnp.int32, (rows * group, 128), 1)
    row = lax.broadcasted_iota(jnp.int32, (rows * group, 128), 0) % rows
    diagonal = lane == jnp.where(row < half, row, row - half + 64) + low_row
    ones = jnp.ones((128, 128), jnp.bfloat16)

    def step(index, carry):
        first = index * group
        spread = jnp.concatenate(
            [jnp.broadcast_to(velocity_ref[pl.ds(first + j, 1), :], (rows, 128)) for j in range(group)], 0
        )
        picked = jnp.where(diagonal, spread, 0.0).astype(jnp.bfloat16)
        speed = jnp.dot(picked, ones, preferred_element_type=jnp.float32)
        angle = speed * const_ref[TERMS : TERMS + 1, :]
        square = angle * angle
        series = jnp.broadcast_to(const_ref[TERMS - 1 : TERMS, :], square.shape)
        for k in range(TERMS - 2, -1, -1):
            series = series * square + const_ref[k : k + 1, :]
        both = series * jnp.where(lane < 64, 1.0, angle)
        trig_ref[pl.ds(first, group)] = both.reshape(group, 2, half, 128)
        return carry

    lax.fori_loop(0, sources // group, step, 0)


def trig_table(velocity, half=16, group=32):
    sources = velocity.shape[0]
    const = jnp.asarray(trig_constants())
    return pl.pallas_call(
        functools.partial(trig_kernel, group=group),
        grid=(64 // half,),
        in_specs=[
            pl.BlockSpec(const.shape, lambda g: (0, 0)),
            pl.BlockSpec(velocity.shape, lambda g: (0, 0)),
        ],
        out_specs=pl.BlockSpec((sources, 2, half, 128), lambda g: (0, 0, g, 0)),
        out_shape=jax.ShapeDtypeStruct((sources, 2, 64, 128), jnp.float32),
        compiler_params=pltpu.CompilerParams(vmem_limit_bytes=24 * 2**20),
        cost_estimate=pl.CostEstimate(flops=4 * 10**9, bytes_accessed=8 * 2**20, transcendentals=0),
    )(const, velocity)


def butterfly_kernel(weights_x, weights_y, trig_ref, in_ref, out_ref, cos_ref, sin_ref, state_ref, *, bits, group):
    sources, _, half, _ = in_ref.shape
    rows = 2 * half
    low = lax.broadcasted_iota(jnp.int32, (group * rows, 128), 1) < 64

    def enter(index, carry):
        first = index * group
        both = trig_ref[pl.ds(first, group)].reshape(group * rows, 128)
        other = swap_parts(both)
        cosine = jnp.where(low, both, other)
        sine = jnp.where(low, other, -both)
        values = in_ref[pl.ds(first, group)].reshape(group * rows, 128).astype(jnp.float32)
        turned = values * cosine + swap_parts(values) * sine
        cos_ref[pl.ds(first, group)] = cosine.reshape(group, rows, 128)
        sin_ref[pl.ds(first, group)] = sine.reshape(group, rows, 128)
        state_ref[pl.ds(first, group)] = turned.astype(jnp.bfloat16).reshape(group, rows, 128)
        return carry

    lax.fori_loop(0, sources // group, enter, 0)

    for level, bit in enumerate(bits):
        matrix = (weights_x, weights_y)[level % 2]
        if bit is not None:
            pairs = []
            for pair in range(sources // 2):
                lower = (pair >> bit) << (bit + 1) | pair & (1 << bit) - 1
                pairs.append((lower, lower + (1 << bit)))
            left = jnp.concatenate([jnp.concatenate([state_ref[a], state_ref[b]], 1) for a, b in pairs], 0)
            joined = jnp.dot(left, matrix[...], preferred_element_type=jnp.float32)
            for place, pair in enumerate(pairs):
                for side, box in enumerate(pair):
                    values = joined[place * rows : (place + 1) * rows, side * 128 : side * 128 + 128]
                    turned = values * cos_ref[box] + swap_parts(values) * sin_ref[box]
                    state_ref[box] = turned.astype(jnp.bfloat16)
        else:
            left = jnp.concatenate(
                [jnp.concatenate([state_ref[a, :half], state_ref[a, half:]], 1) for a in range(sources)], 0
            )
            joined = jnp.dot(left, matrix[...], preferred_element_type=jnp.float32)
            for box in range(sources):
                cosine, sine = cos_ref[box], sin_ref[box]
                for _ in range(3):
                    cosine, sine = cosine * cosine - sine * sine, 2.0 * (cosine * sine)
                part = joined[box * half : (box + 1) * half]
                values = jnp.concatenate([part[:, :128], part[:, 128:]], 0)
                turned = values * cosine - swap_parts(values) * sine
                out_ref[box] = turned.astype(out_ref.dtype).reshape(2, half, 128)


def butterfly(values, trig, matrix_x, matrix_y, chunk, bits, half=16, group=16):
    sources, _, extent, _ = values.shape
    first = chunk * extent // half
    whole = pl.BlockSpec((256, 256), lambda g: (0, 0))
    block = pl.BlockSpec((sources, 2, half, 128), lambda g: (0, 0, g, 0))
    trig_block = pl.BlockSpec((sources, 2, half, 128), lambda g: (0, 0, first + g, 0))
    table = pltpu.VMEM((sources, 2 * half, 128), jnp.float32)
    return pl.pallas_call(
        functools.partial(butterfly_kernel, bits=bits, group=group),
        grid=(extent // half,),
        in_specs=[whole, whole, trig_block, block],
        out_specs=block,
        out_shape=jax.ShapeDtypeStruct(values.shape, jnp.bfloat16),
        scratch_shapes=[table, table, pltpu.VMEM((sources, 2 * half, 128), jnp.bfloat16)],
        compiler_params=pltpu.CompilerParams(vmem_limit_bytes=48 * 2**20),
        cost_estimate=pl.CostEstimate(
            flops=16 * 10**9 * extent // 64, bytes_accessed=16 * 2**20 * extent // 64, transcendentals=0
        ),
    )(matrix_x, matrix_y, trig, values)


def pair_matrix(translation, dim_index):
    blocks = translation[dim_index]
    upper = jnp.concatenate([blocks[:, :, 0], blocks[:, :, 1]], axis=-1)
    lower = jnp.concatenate([-blocks[:, :, 1], blocks[:, :, 0]], axis=-1)
    matrices = jnp.concatenate([upper, lower], axis=-2)
    return matrices.transpose(1, 2, 0, 3).reshape(256, 256)


def exchange(values):
    return lax.all_to_all(values, EVERY, 0, 0, tiled=True)


def shards(weights, velocity, translation):
    bits = level_bits(lax.axis_size("sx"), lax.axis_size("sy"))
    grouped = weights.reshape(128, 2, 64, 128)
    size = 64 // CHUNKS
    speeds = exchange(velocity[:, None, :]).reshape(128, 128).astype(jnp.float32)
    trig = trig_table(speeds)
    matrix_x = pair_matrix(translation, 0)
    matrix_y = pair_matrix(translation, 1)
    results = []
    for chunk in range(CHUNKS):
        arrived = exchange(grouped[:, :, chunk * size : (chunk + 1) * size])
        results.append(exchange(butterfly(arrived, trig, matrix_x, matrix_y, chunk, bits)))
    final = jnp.concatenate([part.astype(jnp.float32) for part in results], axis=2)
    return final.reshape(128, 128, 128)


def solution(mesh):
    placed = (P("sx", "sy", None), P("sx", "sy"), P())
    return jax.shard_map(
        shards, mesh=mesh, in_specs=placed, out_specs=P("sx", "sy", None), check_vma=False
    )
```

time: 931 us -> 173 us (0.19)
  waiting for transfers between devices: 518 us -> 16.3 us
  other arithmetic: 289 us -> 7.66 us
  blocking collectives: 0 us -> 69.1 us
  matrix products: 48.3 us -> 0 us
  Pallas kernels: 0 us -> 39.9 us
  local copies, waits for them, and re-layouts: 45.9 us -> 12.4 us
    ppermute x7 -> x0, waiting for transfers between devices: 518 us -> none  [from_partner(): lax.ppermute(x, axis, [(i, i ^ 1 << stride) for i in range(lax.axis_size(...]
    another operation x10 -> x0, other arithmetic: 244 us -> none
    all_to_all x0 -> x2, blocking collectives: none -> 69.1 us  [exchange(): return lax.all_to_all(values, EVERY, 0, 0, tiled=True)]
    dot_general x18 -> x0, matrix products: 48.3 us -> none  [the longest x7 24.2 us: pair_remote(): jnp.dot(partner, other_matrix, preferred_element_type=jnp.float32)]
    pallas_call x0 -> x3, Pallas kernels: none -> 39.9 us  [the longest x2 32.1 us: butterfly(): pl.pallas_call(functools.partial(butterfly_kernel, bits=bits, group=group...]
    all_to_all x0 -> x3, starting transfers between devices: none -> 27.4 us  [exchange(): return lax.all_to_all(values, EVERY, 0, 0, tiled=True)]
    concatenate x3 -> x0, local copies, waits for them, and re-layouts: 23.1 us -> none  [rotate_phase(): jnp.concatenate([real_part * cosine - imag_part * sine, real_part * sine...]
    ppermute x7 -> x0, starting transfers between devices: 20.4 us -> none  [from_partner(): lax.ppermute(x, axis, [(i, i ^ 1 << stride) for i in range(lax.axis_size(...]
  transfers between devices with their start and end apart: 7 -> 3, of which waited for: 7 -> 2; matrix products, arithmetic and copies ran while one was open for 2% -> 3% of each run, Pallas kernels for 0% -> 23%
where the time goes in v1:
time: 173 us
  blocking collectives  69.1 us (40%)
  Pallas kernels  39.9 us (23%)
  starting transfers between devices  27.4 us (16%)
  waiting for transfers between devices  16.3 us (9%)
  local copies, waits for them, and re-layouts  12.4 us (7%)
  other arithmetic  7.66 us (4%)
    all_to_all x2, blocking collectives, exchange(): return lax.all_to_all(values, EVERY, 0, 0, tiled=True)  69.1 us
    pallas_call x2, Pallas kernels, butterfly(): pl.pallas_call(functools.partial(butterfly_kernel, bits=bits, group=group...  32.1 us
    all_to_all x3, starting transfers between devices, exchange(): return lax.all_to_all(values, EVERY, 0, 0, tiled=True)  27.4 us
    all_to_all x3, waiting for transfers between devices, exchange(): return lax.all_to_all(values, EVERY, 0, 0, tiled=True)  16.3 us
    pallas_call x1, Pallas kernels, trig_table(): pl.pallas_call(functools.partial(trig_kernel, group=group), grid=(64 // h...  7.81 us
    unnamed x14, local copies, waits for them, and re-layouts  6.07 us
    reshape x1, other arithmetic, shards(): return final.reshape(128, 128, 128)  4.75 us
    slice x1, local copies, waits for them, and re-layouts, shards(): arrived = exchange(grouped[:, :, chunk * size:(chunk + 1) * size])  4.57 us
  transfers between devices with their start and end apart: 3, of which 2 were waited for; matrix products, arithmetic and copies ran while one was open for 3% of the time, Pallas kernels for 23%

profile of v1, /device:TPU:1, one launch (start us, length us, event | category | flops | bytes accessed | tf_op | source)
XLA Modules:
  0.0 172.9 jit_solution(10427054292260071901)
XLA Ops:
  0.0 1.4 copy.18
  1.4 11.5 %all-to-all-start = ((bf16[128,1,128]{2,1,0:T(2,128)(2,1)}), bf16[128,1,128]{2,1,0:T(2,128)(2,1)S(1)}, u32[]{:S(2)}, u32[]{:S(2)}) async-start(bf16[128,1,128]{2,1,0:T(2,128)(2,1)} %copy.18), calls=%async_computation | async-start | bytes 131072 | tf_op jit(solution)/shard_map/all_to_all | solution.py:179
  12.9 4.6 %fusion.2 = (bf16[128,2,32,128]{3,2,1,0:T(8,128)(2,1)S(1)}, bf16[128,2,32,128]{3,2,1,0:T(8,128)(2,1)}) fusion(bf16[128,2,64,128]{3,2,1,0:T(8,128)(2,1)} %bitcast.46), kind=kLoop, calls=%fused_computation.15 | loop fusion | bytes 8388608 | tf_op jit(solution)/shard_map/slice | solution.py:192
  17.5 4.8 %all-to-all-done = bf16[128,1,128]{2,1,0:T(2,128)(2,1)S(1)} async-done(((bf16[128,1,128]{2,1,0:T(2,128)(2,1)}), bf16[128,1,128]{2,1,0:T(2,128)(2,1)S(1)}, u32[]{:S(2)}, u32[]{:S(2)}) %all-to-all-start) | async-done | bytes 32800 | tf_op jit(solution)/shard_map/all_to_all | solution.py:179
  22.3 0.0 copy-start.5
  22.3 34.2 %all_to_all.25.in_ref = bf16[128,2,32,128]{3,2,1,0:T(8,128)(2,1)} all-to-all(bf16[128,2,32,128]{3,2,1,0:T(8,128)(2,1)S(1)} %get-tuple-element.5), channel_id=1, replica_groups=mesh['sx'=16,'sy'=8] {'sx','sy'}, dimensions={0} | all-to-all | bytes 4194304 | tf_op jit(solution)/shard_map/all_to_all | solution.py:179
  56.5 0.0 copy-start.3
  56.5 5.6 %all-to-all-start.3 = ((bf16[128,2,32,128]{3,2,1,0:T(8,128)(2,1)}), bf16[128,2,32,128]{3,2,1,0:T(8,128)(2,1)S(1)}, u32[]{:S(2)}, u32[]{:S(2)}) async-start(bf16[128,2,32,128]{3,2,1,0:T(8,128)(2,1)} %get-tuple-element.6), calls=%async_computation.3 | async-start | bytes 4194304 | tf_op jit(solution)/shard_map/all_to_all | solution.py:179
  62.1 0.0 copy-done.5
  62.2 0.1 maximum_bitcast_fusion.1
  62.3 0.1 copy.17
  62.5 0.1 maximum_bitcast_fusion
  62.6 0.1 copy.15
  62.8 0.0 copy-done.3
  62.8 0.0 copy-start
  62.8 7.8 %shard_map.46.trig_ref = f32[128,2,64,128]{3,2,1,0:T(8,128)S(1)} custom-call(f32[8,128]{1,0:T(8,128)S(1)} %copy-done.3, f32[128,128]{1,0:T(8,128)S(1)} %bitcast_convert_fusion.1.velocity_ref), custom_call_target="tpu_custom_call" | custom-call | flops 4000000000 | bytes 8388608 | tf_op jit(solution)/shard_map/pallas_call | solution.py:86
  70.6 0.0 copy-start.4
  70.6 3.4 %copy-done.4 = f32[128,2,64,128]{3,2,1,0:T(8,128)} copy-done((f32[128,2,64,128]{3,2,1,0:T(8,128)}, f32[128,2,64,128]{3,2,1,0:T(8,128)S(1)}, u32[]{:S(2)}) %copy-start.4) | copy-done | bytes 8388632
  74.0 0.0 copy-done
  74.0 16.1 %shard_map.47 = bf16[128,2,32,128]{3,2,1,0:T(8,128)(2,1)S(1)} custom-call(bf16[256,256]{1,0:T(8,128)(2,1)S(1)} %bitcast.44, bf16[256,256]{1,0:T(8,128)(2,1)S(1)} %bitcast.42, f32[128,2,64,128]{3,2,1,0:T(8,128)} %copy-done.4, bf16[128,2,32,128]{3,2,1,0:T(8,128)(2,1)S(1)} %copy-done), custom_call_target="tpu_custom_call" | custom-call | flops 8000000000 | bytes 8388608 | tf_op jit(solution)/shard_map/pallas_call | solution.py:156
  90.1 0.0 copy-start.1
  90.1 1.3 copy-done.1
  91.4 0.0 all-to-all-done.3.in_ref
  91.4 10.2 %all-to-all-start.2 = ((bf16[128,2,32,128]{3,2,1,0:T(8,128)(2,1)}), bf16[128,2,32,128]{3,2,1,0:T(8,128)(2,1)}, u32[]{:S(2)}, u32[]{:S(2)}) async-start(bf16[128,2,32,128]{3,2,1,0:T(8,128)(2,1)} %copy-done.1), calls=%async_computation.2 | async-start | bytes 4194304 | tf_op jit(solution)/shard_map/all_to_all | solution.py:179
  101.7 16.1 %shard_map.48 = bf16[128,2,32,128]{3,2,1,0:T(8,128)(2,1)S(1)} custom-call(bf16[256,256]{1,0:T(8,128)(2,1)S(1)} %bitcast.45, bf16[256,256]{1,0:T(8,128)(2,1)S(1)} %bitcast.43, f32[128,2,64,128]{3,2,1,0:T(8,128)} %copy-done.4, bf16[128,2,32,128]{3,2,1,0:T(8,128)(2,1)S(1)} %all-to-all-done.3.in_ref), custom_call_target="tpu_custom_call" | custom-call | flops 8000000000 | bytes 8388608 | tf_op jit(solution)/shard_map/pallas_call | solution.py:156
  117.7 0.0 copy-start.2
  117.8 1.3 copy-done.2
  119.1 11.5 %all-to-all-done.2 = bf16[128,2,32,128]{3,2,1,0:T(8,128)(2,1)} async-done(((bf16[128,2,32,128]{3,2,1,0:T(8,128)(2,1)}), bf16[128,2,32,128]{3,2,1,0:T(8,128)(2,1)}, u32[]{:S(2)}, u32[]{:S(2)}) %all-to-all-start.2) | async-done | bytes 2097184 | tf_op jit(solution)/shard_map/all_to_all | solution.py:179
  130.6 34.9 %all_to_all.26 = bf16[128,2,32,128]{3,2,1,0:T(8,128)(2,1)S(1)} all-to-all(bf16[128,2,32,128]{3,2,1,0:T(8,128)(2,1)} %copy-done.2), channel_id=1, replica_groups=mesh['sx'=16,'sy'=8] {'sx','sy'}, dimensions={0} | all-to-all | bytes 4194304 | tf_op jit(solution)/shard_map/all_to_all | solution.py:179
  165.5 2.7 %pad_maximum_fusion = bf16[128,2,64,128]{3,2,1,0:T(8,128)(2,1)S(1)} fusion(bf16[128,2,32,128]{3,2,1,0:T(8,128)(2,1)S(1)} %all_to_all.26, bf16[128,2,32,128]{3,2,1,0:T(8,128)(2,1)} %all-to-all-done.2), kind=kLoop, calls=%fused_computation | loop fusion | flops 8388608 | bytes 8388608 | tf_op jit(solution)/shard_map/concatenate | solution.py:194
  168.2 4.7 %bitcast_convert_fusion = f32[128,128,128]{2,1,0:T(8,128)} fusion(bf16[128,2,64,128]{3,2,1,0:T(8,128)(2,1)S(1)} %pad_maximum_fusion), kind=kLoop, calls=%fused_computation.1 | loop fusion | flops 2097152 | bytes 12582912 | tf_op jit(solution)/shard_map/reshape | solution.py:195
  (6 shorter events, 0.1 us)
Async XLA Ops:
  1.4 20.9 %all-to-all-start = ((bf16[128,1,128]{2,1,0:T(2,128)(2,1)}), bf16[128,1,128]{2,1,0:T(2,128)(2,1)S(1)}, u32[]{:S(2)}, u32[]{:S(2)}) async-start(bf16[128,1,128]{2,1,0:T(2,128)(2,1)} %copy.18), calls=%async_computation | async-start | bytes 131072 | tf_op jit(solution)/shard_map/all_to_all | solution.py:179
  22.3 39.8 %copy-start.5 = (bf16[2,2,2,2,64,64]{5,4,3,2,1,0:T(8,128)(2,1)S(1)}, bf16[2,2,2,2,64,64]{5,4,3,2,1,0:T(8,128)(2,1)}, u32[]{:S(2)}) copy-start(bf16[2,2,2,2,64,64]{5,4,3,2,1,0:T(8,128)(2,1)} %param.6) | copy-start | bytes 393220
  56.5 6.3 %copy-start.3 = (f32[8,128]{1,0:T(8,128)S(1)}, f32[8,128]{1,0:T(8,128)}, u32[]{:S(2)}) copy-start(f32[8,128]{1,0:T(8,128)} %constant.2.clone.const_ref) | copy-start | bytes 12292
  56.5 34.9 %all-to-all-start.3 = ((bf16[128,2,32,128]{3,2,1,0:T(8,128)(2,1)}), bf16[128,2,32,128]{3,2,1,0:T(8,128)(2,1)S(1)}, u32[]{:S(2)}, u32[]{:S(2)}) async-start(bf16[128,2,32,128]{3,2,1,0:T(8,128)(2,1)} %get-tuple-element.6), calls=%async_computation.3 | async-start | bytes 4194304 | tf_op jit(solution)/shard_map/all_to_all | solution.py:179
  62.8 11.2 %copy-start = (bf16[128,2,32,128]{3,2,1,0:T(8,128)(2,1)S(1)}, bf16[128,2,32,128]{3,2,1,0:T(8,128)(2,1)}, u32[]{:S(2)}) copy-start(bf16[128,2,32,128]{3,2,1,0:T(8,128)(2,1)} %all_to_all.25.in_ref) | copy-start | bytes 6291460
  70.6 3.4 %copy-start.4 = (f32[128,2,64,128]{3,2,1,0:T(8,128)}, f32[128,2,64,128]{3,2,1,0:T(8,128)S(1)}, u32[]{:S(2)}) copy-start(f32[128,2,64,128]{3,2,1,0:T(8,128)S(1)} %shard_map.46.trig_ref) | copy-start | bytes 25165828
  90.1 1.3 copy-start.1
  91.4 39.2 %all-to-all-start.2 = ((bf16[128,2,32,128]{3,2,1,0:T(8,128)(2,1)}), bf16[128,2,32,128]{3,2,1,0:T(8,128)(2,1)}, u32[]{:S(2)}, u32[]{:S(2)}) async-start(bf16[128,2,32,128]{3,2,1,0:T(8,128)(2,1)} %copy-done.1), calls=%async_computation.2 | async-start | bytes 4194304 | tf_op jit(solution)/shard_map/all_to_all | solution.py:179
  117.7 1.3 copy-start.2

commit v2 on v1

v2 whole, which is shorter than its diff:
```python
import functools

import jax
import jax.numpy as jnp
import numpy as np
from jax import lax
from jax.experimental import pallas as pl
from jax.experimental.pallas import tpu as pltpu
from jax.sharding import PartitionSpec as P

TERMS = 7
MAX_ANGLE = 2.95
HALF = 16
EVERY = ("sx", "sy")
CHUNKS = 2
STRIPS = 2
VMEM_LIMIT = 60 * 2**20


def unit_bits(count_x, count_y):
    bits_x = count_x.bit_length() - 1
    bits_y = count_y.bit_length() - 1
    order = []
    for step in range(bits_x):
        order.append(bits_y + bits_x - step)
        order.append(bits_y - step)
    return order


def half_totals():
    counter = np.arange(8, dtype=np.float64)
    nodes = np.cos(np.pi * (2.0 * counter + 1.0) / 16.0)
    totals = (nodes[:, None] + nodes[None, :]).reshape(64) * 0.5
    return np.concatenate([totals, totals])


def trig_constants():
    top = MAX_ANGLE**2
    count = 400
    square = (np.cos(np.pi * (np.arange(count) + 0.5) / count) + 1) / 2 * top
    angle = np.sqrt(square)

    def fit(values):
        series = np.polynomial.chebyshev.Chebyshev.fit(square, values, TERMS - 1, domain=[0, top])
        return series.convert(kind=np.polynomial.Polynomial, domain=[-1, 1], window=[-1, 1]).coef

    rows = np.zeros((TERMS + 1, 128), np.float32)
    rows[:TERMS, :64] = fit(np.cos(angle))[:, None]
    rows[:TERMS, 64:] = fit(np.sin(angle) / angle)[:, None]
    rows[TERMS] = half_totals()
    return rows


def spread_index(place, bit):
    return (place >> bit) << (bit + 1) | place & (1 << bit) - 1


def drop_bit(unit, bit):
    return (unit >> (bit + 1)) << bit | unit & (1 << bit) - 1


def butterfly_kernel(
    const_ref, speed_ref, split_ref, matrix_x, matrix_y, *refs, bits, wide, group, start
):
    in_refs, out_ref, plain_ref, swapped_ref, states = refs[:2], refs[2], refs[3], refs[4], refs[5:]
    sources, extent, _ = in_refs[0].shape
    half = HALF
    strips = range(extent // half)
    units = 2 * sources
    low = lax.broadcasted_iota(jnp.int32, (half, 128), 1) < 64

    first_row = start + pl.program_id(0) * extent
    lane = lax.broadcasted_iota(jnp.int32, (2 * extent * group, 128), 1)
    row = lax.broadcasted_iota(jnp.int32, (2 * extent * group, 128), 0) % (2 * extent)
    diagonal = lane == jnp.where(row < extent, row, row - extent + 64) + first_row
    ones = jnp.ones((128, 128), jnp.bfloat16)

    def trig(index, carry):
        first = index * group
        spread = jnp.concatenate(
            [jnp.broadcast_to(speed_ref[pl.ds(first + j, 1), :], (2 * extent, 128)) for j in range(group)], 0
        )
        picked = jnp.where(diagonal, spread, 0.0).astype(jnp.bfloat16)
        speed = jnp.dot(picked, ones, preferred_element_type=jnp.float32)
        angle = speed * const_ref[TERMS : TERMS + 1, :]
        square = angle * angle
        series = jnp.broadcast_to(const_ref[TERMS - 1 : TERMS, :], square.shape)
        for k in range(TERMS - 2, -1, -1):
            series = series * square + const_ref[k : k + 1, :]
        both = series * jnp.where(lane < 64, 1.0, angle)
        plain_ref[pl.ds(2 * first, 2 * group)] = both.reshape(2 * group, extent, 128)
        swapped_ref[pl.ds(2 * first, 2 * group)] = pltpu.roll(both, 64, 1).reshape(2 * group, extent, 128)
        return carry

    lax.fori_loop(0, units // 2 // group, trig, 0)

    def tables(first, second, rows):
        cosine = jnp.where(low, plain_ref[first, rows], swapped_ref[second, rows])
        sine = jnp.where(low, swapped_ref[first, rows], plain_ref[second, rows])
        return cosine, sine

    def emit(chosen, left, matrix, finish):
        for begin in range(0, len(chosen), wide):
            joined = jnp.dot(
                jnp.concatenate(left[begin : begin + wide], 0), matrix, preferred_element_type=jnp.float32
            )
            for k, pair in enumerate(chosen[begin : begin + wide]):
                part = joined[k * half : (k + 1) * half]
                finish(pair, part[:, :128], part[:, 128:])

    def turn_back(target, place, rows, real, imag, cosine, sine):
        re_ref, im_ref = target
        re_ref[place, rows] = (real * cosine + imag * sine).astype(jnp.bfloat16)
        im_ref[place, rows] = (imag * cosine - real * sine).astype(jnp.bfloat16)

    pairs = [(spread_index(p, bits[0]), spread_index(p, bits[0]) + (1 << bits[0])) for p in range(units // 2)]
    for strip in strips:
        rows = slice(strip * half, (strip + 1) * half)
        left = [
            jnp.concatenate([in_refs[a % 2][a // 2, rows], in_refs[b % 2][b // 2, rows]], 1) for a, b in pairs
        ]

        def enter(pair, real, imag, rows=rows):
            turn_back(states[:2], drop_bit(pair[0], bits[0]), rows, real, imag, *tables(*pair, rows))

        emit(pairs, left, split_ref[...], enter)

    for level, bit in enumerate(bits):
        before = bits[level - 1] if level else None
        after = bits[level + 1] if level + 1 < len(bits) else None
        now, later = states[2 * (level % 2) :][:2], states[2 * ((level + 1) % 2) :][:2]
        for strip in strips:
            rows = slice(strip * half, (strip + 1) * half)
            for was in range(2 if level else 1):
                for will in range(2 if after is not None else 1):
                    chosen, left = [], []
                    for p in range(units // 2):
                        a = spread_index(p, bit)
                        b = a + (1 << bit)
                        if before is not None and (a >> before) & 1 != was:
                            continue
                        if after is not None and (a >> after) & 1 != will:
                            continue
                        chosen.append((a, b))
                        if before is None:
                            left.append(jnp.concatenate([now[0][p, rows], now[1][p, rows]], 1))
                        else:
                            i, j = drop_bit(a, before), drop_bit(b, before)
                            if was:
                                i, j = j, i
                            left.append(
                                jnp.concatenate([jnp.where(low, part[i, rows], part[j, rows]) for part in now], 1)
                            )

                    def leave(pair, real, imag, rows=rows, will=will, bit=bit, after=after, later=later):
                        a, b = pair
                        cosine, sine = tables(b, a, rows) if will else tables(a, b, rows)
                        if after is not None:
                            turn_back(later, drop_bit(a, bit), rows, real, imag, cosine, sine)
                            return
                        for _ in range(3):
                            cosine, sine = cosine * cosine - sine * sine, 2.0 * (cosine * sine)
                        out_ref[a // 2, 0, rows] = (real * cosine - imag * sine).astype(jnp.bfloat16)
                        out_ref[a // 2, 1, rows] = (imag * cosine + real * sine).astype(jnp.bfloat16)

                    emit(chosen, left, (matrix_x, matrix_y)[level % 2][was, will], leave)


def butterfly(values, speed, start, extent, split, matrices, bits, wide=32, strips=STRIPS, group=16):
    sources = values.shape[0]
    size = strips * HALF
    blocks = extent // size
    const = jnp.asarray(trig_constants())
    inputs = [
        pl.BlockSpec((sources, size, 128), lambda g, part=part: (0, part * blocks + g, 0)) for part in range(2)
    ]
    state = pltpu.VMEM((sources, size, 128), jnp.bfloat16)
    table = pltpu.VMEM((2 * sources, size, 128), jnp.float32)
    return pl.pallas_call(
        functools.partial(butterfly_kernel, bits=bits, wide=wide, group=group, start=start),
        grid=(blocks,),
        in_specs=[
            pl.BlockSpec(const.shape, lambda g: (0, 0)),
            pl.BlockSpec(speed.shape, lambda g: (0, 0)),
            pl.BlockSpec(split.shape, lambda g: (0, 0)),
            pl.BlockSpec((2, 2, 256, 256), lambda g: (0, 0, 0, 0)),
            pl.BlockSpec((2, 2, 256, 256), lambda g: (0, 0, 0, 0)),
            *inputs,
        ],
        out_specs=pl.BlockSpec((sources, 2, size, 128), lambda g: (0, 0, g, 0)),
        out_shape=jax.ShapeDtypeStruct((sources, 2, extent, 128), jnp.bfloat16),
        scratch_shapes=[table, table] + [state] * 4,
        compiler_params=pltpu.CompilerParams(vmem_limit_bytes=VMEM_LIMIT),
        cost_estimate=pl.CostEstimate(
            flops=14 * 10**9 * extent // 64, bytes_accessed=8 * 2**20 * extent // 64, transcendentals=0
        ),
    )(const, speed, split, *matrices, values, values)


def finish_kernel(in_ref, *refs):
    out_ref = refs[-1]
    low = lax.broadcasted_iota(jnp.int32, (1, 128), 1) < 64
    for j in range(out_ref.shape[0]):
        real, imag = in_ref[j, 0].astype(jnp.float32), in_ref[j, 1].astype(jnp.float32)
        out_ref[j, 0] = jnp.where(low, real, pltpu.roll(imag, 64, 1))
        out_ref[j, 1] = jnp.where(low, pltpu.roll(real, 64, 1), imag)


def finish(values, chunk, output, group=32):
    boxes, _, extent, _ = values.shape
    earlier = [] if output is None else [output]
    return pl.pallas_call(
        finish_kernel,
        grid=(boxes // group,),
        in_specs=[pl.BlockSpec((group, 2, extent, 128), lambda g: (g, 0, 0, 0))]
        + [pl.BlockSpec(memory_space=pl.ANY)] * len(earlier),
        out_specs=pl.BlockSpec((group, 2, extent, 128), lambda g: (g, 0, chunk, 0)),
        out_shape=jax.ShapeDtypeStruct((boxes, 2, CHUNKS * extent, 128), jnp.float32),
        input_output_aliases={1: 0} if earlier else {},
        compiler_params=pltpu.CompilerParams(vmem_limit_bytes=24 * 2**20),
        cost_estimate=pl.CostEstimate(flops=10**7, bytes_accessed=6 * 2**20, transcendentals=0),
    )(values, *earlier)


def pair_matrices(translation):
    real, imag = translation[:, :, 0], translation[:, :, 1]
    blocks = jnp.stack([jnp.stack([real, imag]), jnp.stack([-imag, real])])
    blocks = blocks.transpose(0, 3, 4, 1, 2, 5)
    rows = jnp.stack([blocks, blocks[:, ::-1]])
    both = jnp.stack([rows, rows[:, :, :, :, :, ::-1]], 1)
    return both.reshape(2, 2, 256, 256)


def split_matrix():
    out = np.zeros((256, 256), np.float32)
    for box in range(2):
        for part in range(2):
            for t in range(64):
                out[box * 128 + part * 64 + t, part * 128 + box * 64 + t] = 1
    return jnp.asarray(out, jnp.bfloat16)


def exchange(values):
    return lax.all_to_all(values, EVERY, 0, 0, tiled=True)


def shards(weights, velocity, translation):
    bits = unit_bits(lax.axis_size("sx"), lax.axis_size("sy"))
    boxes = weights.shape[0]
    size = 64 // CHUNKS
    rows = 2 * size
    grouped = weights.reshape(boxes, 2, CHUNKS, size, 128)
    split = split_matrix()
    matrices = [pair_matrices(translation[dim]) for dim in range(2)]
    extra = jnp.broadcast_to(velocity[:, None], (boxes, 8, 128))
    first = grouped[:, :, 0].reshape(boxes, rows, 128)
    arrived = [exchange(jnp.concatenate([first, extra], 1))]
    second = grouped[:, :, 1].reshape(boxes, rows, 128)
    arrived[0], second, matrices, split = lax.optimization_barrier((arrived[0], second, matrices, split))
    arrived.append(exchange(second))
    speed = arrived[0][:, rows].astype(jnp.float32)
    back = []
    for chunk in range(CHUNKS):
        done = butterfly(arrived[chunk], speed, chunk * size, size, split, matrices, bits)
        back.append(exchange(done))
    output = None
    for chunk in range(CHUNKS):
        if chunk:
            back[chunk], output = lax.optimization_barrier((back[chunk], output))
        output = finish(back[chunk], chunk, output)
    return output.reshape(weights.shape)


def solution(mesh):
    placed = (P("sx", "sy", None), P("sx", "sy"), P())
    return jax.shard_map(
        shards, mesh=mesh, in_specs=placed, out_specs=P("sx", "sy", None), check_vma=False
    )
```

time: 173 us -> 160 us (0.925)
  blocking collectives: 69.1 us -> 0 us
  waiting for transfers between devices: 16.3 us -> 61.2 us
  local copies, waits for them, and re-layouts: 12.4 us -> 17.4 us
  Pallas kernels: 39.9 us -> 42.4 us
  starting transfers between devices: 27.4 us -> 29.3 us
    all_to_all x2 -> x0, blocking collectives: 69.1 us -> none  [exchange(): return lax.all_to_all(values, EVERY, 0, 0, tiled=True)]
    all_to_all x3 -> x4, waiting for transfers between devices: 16.3 us -> 61.2 us  [exchange(): return lax.all_to_all(values, EVERY, 0, 0, tiled=True)]
    another operation x0 -> x8, other arithmetic: none -> 6.5 us  [the longest x4 3.71 us: pair_matrices(): rows = jnp.stack([blocks, blocks[:, ::-1]])]
    unnamed x14 -> x8, local copies, waits for them, and re-layouts: 6.07 us -> 0.02 us
    rev x0 -> x8, local copies, waits for them, and re-layouts: none -> 5.95 us  [the longest x4 3.01 us: pair_matrices(): both = jnp.stack([rows, rows[:, :, :, :, :, ::-1]], 1)]
    another operation x0 -> x9, local copies, waits for them, and re-layouts: none -> 4.87 us  [the longest x6 3.47 us: pair_matrices(): rows = jnp.stack([blocks, blocks[:, ::-1]])]
    reshape x1 -> x0, other arithmetic: 4.75 us -> none  [shards(): return final.reshape(128, 128, 128)]
    pallas_call x3 -> x4, Pallas kernels: 39.9 us -> 42.4 us  [the longest x2 35.2 us: butterfly(): pl.pallas_call(functools.partial(butterfly_kernel, bits=bits, wide=wide,...]
  transfers between devices with their start and end apart: 3 -> 4, of which waited for: 2 -> 4; matrix products, arithmetic and copies ran while one was open for 3% -> 13% of each run, Pallas kernels for 23% -> 24%
where the time goes in v2:
time: 160 us; the launch traced here: 159 us
  waiting for transfers between devices  61.2 us (38%)
  Pallas kernels  42.4 us (26%)
  starting transfers between devices  29.3 us (18%)
  local copies, waits for them, and re-layouts  17.4 us (11%)
  other arithmetic  8.85 us (6%)
    all_to_all x4, waiting for transfers between devices, exchange(): return lax.all_to_all(values, EVERY, 0, 0, tiled=True)  61.2 us
    pallas_call x2, Pallas kernels, butterfly(): pl.pallas_call(functools.partial(butterfly_kernel, bits=bits, wide=wide,...  35.2 us
    all_to_all x4, starting transfers between devices, exchange(): return lax.all_to_all(values, EVERY, 0, 0, tiled=True)  29.3 us
    pallas_call x2, Pallas kernels, finish(): pl.pallas_call(finish_kernel, grid=(boxes // group,), in_specs=[pl.BlockS...  7.23 us
    slice x1, local copies, waits for them, and re-layouts, shards(): second = grouped[:, :, 1].reshape(boxes, rows, 128)  4.58 us
    another operation x4, other arithmetic, pair_matrices(): rows = jnp.stack([blocks, blocks[:, ::-1]])  3.71 us
    another operation x6, local copies, waits for them, and re-layouts, pair_matrices(): rows = jnp.stack([blocks, blocks[:, ::-1]])  3.47 us
  transfers between devices with their start and end apart: 4, of which 4 were waited for; matrix products, arithmetic and copies ran while one was open for 13% of the time, Pallas kernels for 24%

profile of v2, /device:TPU:1, one launch (start us, length us, event | category | flops | bytes accessed | tf_op | source)
XLA Modules:
  0.0 159.3 jit_solution(869643069109600444)
XLA Ops:
  0.0 0.0 copy-start.3
  0.0 4.6 %fusion.6 = (bf16[128,2,1,32,128]{4,3,2,1,0:T(8,128)(2,1)}, bf16[128,2,1,32,128]{4,3,2,1,0:T(8,128)(2,1)S(1)}) fusion(bf16[128,2,2,32,128]{4,3,2,1,0:T(8,128)(2,1)} %bitcast.52), kind=kLoop, calls=%fused_computation.26 | loop fusion | bytes 8388608 | tf_op jit(solution)/shard_map/slice | solution.py:258
  4.6 0.0 copy-done.3
  4.6 1.7 %pad_maximum_fusion = bf16[128,72,128]{2,1,0:T(8,128)(2,1)} fusion(bf16[128,8,128]{2,1,0:T(8,128)(2,1)S(1)} %broadcast_in_dim.2, bf16[128,64,128]{2,1,0:T(8,128)(2,1)S(1)} %bitcast.51), kind=kLoop, calls=%fused_computation | loop fusion | flops 4718592 | bytes 4718592 | tf_op jit(solution)/shard_map/concatenate | solution.py:257
  6.3 0.0 copy-start.2
  6.3 11.5 %all-to-all-start = ((bf16[128,72,128]{2,1,0:T(8,128)(2,1)}), bf16[128,72,128]{2,1,0:T(8,128)(2,1)S(1)}, u32[]{:S(2)}, u32[]{:S(2)}) async-start(bf16[128,72,128]{2,1,0:T(8,128)(2,1)} %pad_maximum_fusion), calls=%async_computation | async-start | bytes 4718592 | tf_op jit(solution)/shard_map/all_to_all | solution.py:244
  17.8 0.0 copy-done.2
  17.9 0.1 maximum_bitcast_fusion
  18.0 0.8 fusion.2
  18.7 0.7 rev.12
  19.4 1.0 copy.11
  20.4 0.1 maximum_bitcast_fusion.2
  20.5 0.8 fusion
  21.2 0.7 rev.14
  22.0 1.0 copy.15
  22.9 0.0 copy-start.1
  23.0 1.1 pad_maximum_fusion.1
  24.1 0.8 rev.13
  24.9 1.6 copy.13
  26.5 1.0 stack.87
  27.6 1.2 stack.81
  28.7 0.0 copy-done.1
  28.7 0.3 copy.12
  29.0 0.9 stack.82
  29.9 1.1 pad_maximum_fusion.3
  31.0 0.5 copy.17
  31.6 0.3 stack.100
  31.9 1.2 stack.94
  33.1 1.2 copy.16
  34.3 0.2 stack.95
  34.6 1.8 %pad_maximum_fusion.2.matrix_x = bf16[2,2,256,256]{3,2,1,0:T(8,128)(2,1)} fusion(bf16[2,1,256,256]{3,2,1,0:T(8,128)(2,1)} %stack.87, bf16[1,1,256,256]{3,2,1,0:T(8,128)(2,1)} %stack.82, bf16[1,1,256,256]{3,2,1,0:T(8,128)(2,1)S(1)} %stack.81), kind=kLoop, calls=%fused_computation.2 | loop fusion | flops 524288 | bytes 1048576 | tf_op jit(solution)/shard_map/stack | solution.py:230
  36.4 0.8 pad_maximum_fusion.4.matrix_y
  37.2 12.7 %all-to-all-done.refs_0_.refs_1_ = bf16[128,72,128]{2,1,0:T(8,128)(2,1)S(1)} async-done(((bf16[128,72,128]{2,1,0:T(8,128)(2,1)}), bf16[128,72,128]{2,1,0:T(8,128)(2,1)S(1)}, u32[]{:S(2)}, u32[]{:S(2)}) %all-to-all-start) | async-done | bytes 2359328 | tf_op jit(solution)/shard_map/all_to_all | solution.py:244
  49.9 0.0 copy-start
  49.9 6.1 %all-to-all-start.1 = ((bf16[128,64,128]{2,1,0:T(8,128)(2,1)}), bf16[128,64,128]{2,1,0:T(8,128)(2,1)}, u32[]{:S(2)}, u32[]{:S(2)}) async-start(bf16[128,64,128]{2,1,0:T(8,128)(2,1)} %bitcast.2), calls=%async_computation.1 | async-start | bytes 4194304 | tf_op jit(solution)/shard_map/all_to_all | solution.py:244
  56.0 0.7 slice_convert_fusion
  56.6 0.0 copy-done
  56.6 17.6 %shard_map.65 = bf16[128,2,32,128]{3,2,1,0:T(8,128)(2,1)} custom-call(f32[8,128]{1,0:T(8,128)} %constant.5.clone.const_ref, f32[128,128]{1,0:T(8,128)} %bitcast.53, bf16[256,256]{1,0:T(8,128)(2,1)} %constant.4.clone.split_ref, bf16[2,2,256,256]{3,2,1,0:T(8,128)(2,1)} %pad_maximum_fusion.2.matrix_x, bf16[2,2,256,256]{3,2,1,0:T(8,128)(2,1)} %pad_maximum_fusion.4.matrix_y, ...), custom_call_target="tpu_custom_call" | custom-call | flops 7000000000 | bytes 4194304 | tf_op jit(solution)/shard_map/pallas_call | solution.py:179
  74.2 10.7 %all-to-all-done.1.refs_0_.refs_1_ = bf16[128,64,128]{2,1,0:T(8,128)(2,1)} async-done(((bf16[128,64,128]{2,1,0:T(8,128)(2,1)}), bf16[128,64,128]{2,1,0:T(8,128)(2,1)}, u32[]{:S(2)}, u32[]{:S(2)}) %all-to-all-start.1) | async-done | bytes 2097184 | tf_op jit(solution)/shard_map/all_to_all | solution.py:244
  84.9 5.6 %all-to-all-start.3 = ((bf16[128,2,32,128]{3,2,1,0:T(8,128)(2,1)}), bf16[128,2,32,128]{3,2,1,0:T(8,128)(2,1)S(1)}, u32[]{:S(2)}, u32[]{:S(2)}) async-start(bf16[128,2,32,128]{3,2,1,0:T(8,128)(2,1)} %shard_map.65), calls=%async_computation.3 | async-start | bytes 4194304 | tf_op jit(solution)/shard_map/all_to_all | solution.py:244
  90.5 17.6 %shard_map.64 = bf16[128,2,32,128]{3,2,1,0:T(8,128)(2,1)} custom-call(f32[8,128]{1,0:T(8,128)} %constant.5.clone.const_ref, f32[128,128]{1,0:T(8,128)} %bitcast.54, bf16[256,256]{1,0:T(8,128)(2,1)} %constant.4.clone.split_ref, bf16[2,2,256,256]{3,2,1,0:T(8,128)(2,1)} %pad_maximum_fusion.2.matrix_x, bf16[2,2,256,256]{3,2,1,0:T(8,128)(2,1)} %pad_maximum_fusion.4.matrix_y, ...), custom_call_target="tpu_custom_call" | custom-call | flops 7000000000 | bytes 4194304 | tf_op jit(solution)/shard_map/pallas_call | solution.py:179
  108.2 11.7 %all-to-all-done.3.in_ref = bf16[128,2,32,128]{3,2,1,0:T(8,128)(2,1)S(1)} async-done(((bf16[128,2,32,128]{3,2,1,0:T(8,128)(2,1)}), bf16[128,2,32,128]{3,2,1,0:T(8,128)(2,1)S(1)}, u32[]{:S(2)}, u32[]{:S(2)}) %all-to-all-start.3) | async-done | bytes 2097184 | tf_op jit(solution)/shard_map/all_to_all | solution.py:244
  119.8 6.1 %all-to-all-start.2 = ((bf16[128,2,32,128]{3,2,1,0:T(8,128)(2,1)}), bf16[128,2,32,128]{3,2,1,0:T(8,128)(2,1)}, u32[]{:S(2)}, u32[]{:S(2)}) async-start(bf16[128,2,32,128]{3,2,1,0:T(8,128)(2,1)} %shard_map.64), calls=%async_computation.2 | async-start | bytes 4194304 | tf_op jit(solution)/shard_map/all_to_all | solution.py:244
  125.9 2.7 %shard_map.66.refs_0_ = f32[128,2,64,128]{3,2,1,0:T(8,128)} custom-call(bf16[128,2,32,128]{3,2,1,0:T(8,128)(2,1)S(1)} %all-to-all-done.3.in_ref), custom_call_target="tpu_custom_call" | custom-call | flops 10000000 | bytes 6291456 | tf_op jit(solution)/shard_map/pallas_call | solution.py:212
  128.7 26.2 %all-to-all-done.2.in_ref = bf16[128,2,32,128]{3,2,1,0:T(8,128)(2,1)} async-done(((bf16[128,2,32,128]{3,2,1,0:T(8,128)(2,1)}), bf16[128,2,32,128]{3,2,1,0:T(8,128)(2,1)}, u32[]{:S(2)}, u32[]{:S(2)}) %all-to-all-start.2) | async-done | bytes 2097184 | tf_op jit(solution)/shard_map/all_to_all | solution.py:244
  154.8 4.5 %shard_map.67 = f32[128,2,64,128]{3,2,1,0:T(8,128)} custom-call(bf16[128,2,32,128]{3,2,1,0:T(8,128)(2,1)} %all-to-all-done.2.in_ref, f32[128,2,64,128]{3,2,1,0:T(8,128)} %shard_map.66.refs_0_), custom_call_target="tpu_custom_call", output_to_operand_aliasing={{}: (1, {})} | custom-call | flops 10000000 | bytes 6291456 | tf_op jit(solution)/shard_map/pallas_call | solution.py:212
  (7 shorter events, 0.2 us)
Async XLA Ops:
  0.0 4.6 %copy-start.3 = (bf16[128,128]{1,0:T(8,128)(2,1)S(1)}, bf16[128,128]{1,0:T(8,128)(2,1)}, u32[]{:S(2)}) copy-start(bf16[128,128]{1,0:T(8,128)(2,1)} %param.7) | copy-start | bytes 98308
  6.3 11.5 %copy-start.2 = (bf16[2,2,2,2,64,64]{5,4,3,2,1,0:T(8,128)(2,1)S(1)}, bf16[2,2,2,2,64,64]{5,4,3,2,1,0:T(8,128)(2,1)}, u32[]{:S(2)}) copy-start(bf16[2,2,2,2,64,64]{5,4,3,2,1,0:T(8,128)(2,1)} %param.8) | copy-start | bytes 393220
  6.3 43.6 %all-to-all-start = ((bf16[128,72,128]{2,1,0:T(8,128)(2,1)}), bf16[128,72,128]{2,1,0:T(8,128)(2,1)S(1)}, u32[]{:S(2)}, u32[]{:S(2)}) async-start(bf16[128,72,128]{2,1,0:T(8,128)(2,1)} %pad_maximum_fusion), calls=%async_computation | async-start | bytes 4718592 | tf_op jit(solution)/shard_map/all_to_all | solution.py:244
  22.9 5.8 %copy-start.1 = (bf16[2,2,64,2,2,64]{5,2,1,4,3,0:T(8,128)(2,1)S(1)}, bf16[2,2,64,2,2,64]{5,2,1,4,3,0:T(8,128)(2,1)}, u32[]{:S(2)}) copy-start(bf16[2,2,64,2,2,64]{5,2,1,4,3,0:T(8,128)(2,1)} %rev.12) | copy-start | bytes 393220
  49.9 6.7 %copy-start = (bf16[128,72,128]{2,1,0:T(8,128)(2,1)}, bf16[128,72,128]{2,1,0:T(8,128)(2,1)S(1)}, u32[]{:S(2)}) copy-start(bf16[128,72,128]{2,1,0:T(8,128)(2,1)S(1)} %all-to-all-done.refs_0_.refs_1_) | copy-start | bytes 7077892
  49.9 35.0 %all-to-all-start.1 = ((bf16[128,64,128]{2,1,0:T(8,128)(2,1)}), bf16[128,64,128]{2,1,0:T(8,128)(2,1)}, u32[]{:S(2)}, u32[]{:S(2)}) async-start(bf16[128,64,128]{2,1,0:T(8,128)(2,1)} %bitcast.2), calls=%async_computation.1 | async-start | bytes 4194304 | tf_op jit(solution)/shard_map/all_to_all | solution.py:244
  84.9 34.9 %all-to-all-start.3 = ((bf16[128,2,32,128]{3,2,1,0:T(8,128)(2,1)}), bf16[128,2,32,128]{3,2,1,0:T(8,128)(2,1)S(1)}, u32[]{:S(2)}, u32[]{:S(2)}) async-start(bf16[128,2,32,128]{3,2,1,0:T(8,128)(2,1)} %shard_map.65), calls=%async_computation.3 | async-start | bytes 4194304 | tf_op jit(solution)/shard_map/all_to_all | solution.py:244
  119.8 35.0 %all-to-all-start.2 = ((bf16[128,2,32,128]{3,2,1,0:T(8,128)(2,1)}), bf16[128,2,32,128]{3,2,1,0:T(8,128)(2,1)}, u32[]{:S(2)}, u32[]{:S(2)}) async-start(bf16[128,2,32,128]{3,2,1,0:T(8,128)(2,1)} %shard_map.64), calls=%async_computation.2 | async-start | bytes 4194304 | tf_op jit(solution)/shard_map/all_to_all | solution.py:244

commit v3 on v2

--- a/solution.py
+++ b/solution.py
@@ -206,7 +206,7 @@
         out_ref[j, 1] = jnp.where(low, pltpu.roll(real, 64, 1), imag)
 
 
-def finish(values, chunk, output, group=32):
+def finish(values, chunk, output, group=64):
     boxes, _, extent, _ = values.shape
     earlier = [] if output is None else [output]
     return pl.pallas_call(
@@ -249,13 +249,13 @@
     boxes = weights.shape[0]
     size = 64 // CHUNKS
     rows = 2 * size
-    grouped = weights.reshape(boxes, 2, CHUNKS, size, 128)
     split = split_matrix()
     matrices = [pair_matrices(translation[dim]) for dim in range(2)]
     extra = jnp.broadcast_to(velocity[:, None], (boxes, 8, 128))
-    first = grouped[:, :, 0].reshape(boxes, rows, 128)
-    arrived = [exchange(jnp.concatenate([first, extra], 1))]
-    second = grouped[:, :, 1].reshape(boxes, rows, 128)
+    first = jnp.concatenate([weights[:, :size], weights[:, 64 : 64 + size], extra], 1)
+    first, weights = lax.optimization_barrier((first, weights))
+    arrived = [exchange(first)]
+    second = jnp.concatenate([weights[:, size:64], weights[:, 64 + size :]], 1)
     arrived[0], second, matrices, split = lax.optimization_barrier((arrived[0], second, matrices, split))
     arrived.append(exchange(second))
     speed = arrived[0][:, rows].astype(jnp.float32)

time: 160 us -> 157 us (0.981)
  waiting for transfers between devices: 61.2 us -> 58 us
    all_to_all x4, waiting for transfers between devices: 61.2 us -> 58 us  [exchange(): return lax.all_to_all(values, EVERY, 0, 0, tiled=True)]
    concatenate x1 -> x2, other arithmetic: 1.67 us -> 3.22 us  [the longest x1 1.64 us: shards(): jnp.concatenate([weights[:, :size], weights[:, 64:64 + size], extra], 1)]
    slice x1 -> x2, local copies, waits for them, and re-layouts: 4.58 us -> 3.86 us  [the longest x1 1.93 us: shards(): weights[:, :size]]
  transfers between devices with their start and end apart: 4 -> 4, of which waited for: 4 -> 4; matrix products, arithmetic and copies ran while one was open for 13% -> 15% of each run, Pallas kernels for 24% -> 24%
where the time goes in v3:
time: 157 us; the launch traced here: 156 us
  waiting for transfers between devices  58 us (37%)
  Pallas kernels  41.2 us (26%)
  starting transfers between devices  29.3 us (19%)
  local copies, waits for them, and re-layouts  16.7 us (11%)
  other arithmetic  10.4 us (7%)
    all_to_all x4, waiting for transfers between devices, exchange(): return lax.all_to_all(values, EVERY, 0, 0, tiled=True)  58 us
    pallas_call x2, Pallas kernels, butterfly(): pl.pallas_call(functools.partial(butterfly_kernel, bits=bits, wide=wide,...  35.2 us
    all_to_all x4, starting transfers between devices, exchange(): return lax.all_to_all(values, EVERY, 0, 0, tiled=True)  29.3 us
    pallas_call x2, Pallas kernels, finish(): pl.pallas_call(finish_kernel, grid=(boxes // group,), in_specs=[pl.BlockS...  6.02 us
    another operation x4, other arithmetic, pair_matrices(): rows = jnp.stack([blocks, blocks[:, ::-1]])  3.73 us
    another operation x6, local copies, waits for them, and re-layouts, pair_matrices(): rows = jnp.stack([blocks, blocks[:, ::-1]])  3.48 us
  transfers between devices with their start and end apart: 4, of which 4 were waited for; matrix products, arithmetic and copies ran while one was open for 15% of the time, Pallas kernels for 24%

profile of v3, /device:TPU:1, one launch (start us, length us, event | category | flops | bytes accessed | tf_op | source)
XLA Modules:
  0.0 155.8 jit_solution(2180604327396519334)
XLA Ops:
  0.0 0.0 copy-start.3
  0.0 1.9 %fusion.7 = (bf16[128,32,128]{2,1,0:T(8,128)(2,1)S(1)}, bf16[128,32,128]{2,1,0:T(8,128)(2,1)S(1)}) fusion(bf16[128,128,128]{2,1,0:T(8,128)(2,1)} %param.6), kind=kLoop, calls=%fused_computation.28 | loop fusion | bytes 4194304 | tf_op jit(solution)/shard_map/slice | solution.py:255
  1.9 0.0 copy-done.3
  2.0 1.6 %pad_maximum_fusion = bf16[128,72,128]{2,1,0:T(8,128)(2,1)} fusion(bf16[128,8,128]{2,1,0:T(8,128)(2,1)S(1)} %broadcast_in_dim.2, bf16[128,32,128]{2,1,0:T(8,128)(2,1)S(1)} %get-tuple-element.26, bf16[128,32,128]{2,1,0:T(8,128)(2,1)S(1)} %get-tuple-element.25), kind=kLoop, calls=%fused_computation | loop fusion | flops 7077888 | bytes 4718592 | tf_op jit(solution)/shard_map/concatenate | solution.py:255
  3.6 0.0 copy-start.2
  3.6 11.5 %all-to-all-start = ((bf16[128,72,128]{2,1,0:T(8,128)(2,1)}), bf16[128,72,128]{2,1,0:T(8,128)(2,1)S(1)}, u32[]{:S(2)}, u32[]{:S(2)}) async-start(bf16[128,72,128]{2,1,0:T(8,128)(2,1)} %pad_maximum_fusion), calls=%async_computation | async-start | bytes 4718592 | tf_op jit(solution)/shard_map/all_to_all | solution.py:244
  15.1 0.0 copy-done.2
  15.2 0.1 maximum_bitcast_fusion
  15.3 0.8 fusion.2
  16.1 0.7 rev.12
  16.8 1.0 copy.9
  17.7 0.1 maximum_bitcast_fusion.2
  17.8 0.8 fusion
  18.6 0.7 rev.14
  19.3 1.0 copy.13
  20.3 0.0 copy-start.1
  20.3 1.1 pad_maximum_fusion.2
  21.4 0.8 rev.13
  22.3 1.6 %copy.11 = bf16[2,2,2,64,2,2,64]{6,5,4,3,2,1,0:T(2,128)(2,1)S(1)} copy(bf16[2,2,2,64,2,2,64]{6,3,2,5,4,1,0:T(8,128)(2,1)} %rev.13) | data formatting | bytes 524288 | tf_op jit(solution)/shard_map/rev | solution.py:230
  23.8 1.0 stack.87
  24.9 1.2 stack.81
  26.1 0.0 copy-done.1
  26.1 0.3 copy.10
  26.4 0.9 stack.82
  27.3 1.1 pad_maximum_fusion.4
  28.4 0.5 copy.15
  28.9 0.3 stack.100
  29.3 1.2 stack.94
  30.5 1.2 copy.14
  31.7 0.2 stack.95
  31.9 1.8 %pad_maximum_fusion.3.matrix_x = bf16[2,2,256,256]{3,2,1,0:T(8,128)(2,1)} fusion(bf16[2,1,256,256]{3,2,1,0:T(8,128)(2,1)} %stack.87, bf16[1,1,256,256]{3,2,1,0:T(8,128)(2,1)} %stack.82, bf16[1,1,256,256]{3,2,1,0:T(8,128)(2,1)S(1)} %stack.81), kind=kLoop, calls=%fused_computation.3 | loop fusion | flops 524288 | bytes 1048576 | tf_op jit(solution)/shard_map/stack | solution.py:230
  33.7 0.9 pad_maximum_fusion.5.matrix_y
  34.6 1.9 %fusion.6 = (bf16[128,32,128]{2,1,0:T(8,128)(2,1)S(1)}, bf16[128,32,128]{2,1,0:T(8,128)(2,1)S(1)}) fusion(bf16[128,128,128]{2,1,0:T(8,128)(2,1)} %param.6), kind=kLoop, calls=%fused_computation.27 | loop fusion | bytes 4194304 | tf_op jit(solution)/shard_map/slice | solution.py:258
  36.5 1.6 %pad_maximum_fusion.1 = bf16[128,64,128]{2,1,0:T(8,128)(2,1)} fusion(bf16[128,32,128]{2,1,0:T(8,128)(2,1)S(1)} %get-tuple-element.24, bf16[128,32,128]{2,1,0:T(8,128)(2,1)S(1)} %get-tuple-element.23), kind=kLoop, calls=%fused_computation.1 | loop fusion | flops 4194304 | bytes 4194304 | tf_op jit(solution)/shard_map/concatenate | solution.py:258
  38.1 9.1 %all-to-all-done.refs_0_.refs_1_ = bf16[128,72,128]{2,1,0:T(8,128)(2,1)S(1)} async-done(((bf16[128,72,128]{2,1,0:T(8,128)(2,1)}), bf16[128,72,128]{2,1,0:T(8,128)(2,1)S(1)}, u32[]{:S(2)}, u32[]{:S(2)}) %all-to-all-start) | async-done | bytes 2359328 | tf_op jit(solution)/shard_map/all_to_all | solution.py:244
  47.2 0.0 copy-start
  47.2 6.1 %all-to-all-start.1 = ((bf16[128,64,128]{2,1,0:T(8,128)(2,1)}), bf16[128,64,128]{2,1,0:T(8,128)(2,1)}, u32[]{:S(2)}, u32[]{:S(2)}) async-start(bf16[128,64,128]{2,1,0:T(8,128)(2,1)} %pad_maximum_fusion.1), calls=%async_computation.1 | async-start | bytes 4194304 | tf_op jit(solution)/shard_map/all_to_all | solution.py:244
  53.3 0.7 slice_convert_fusion
  54.0 0.0 copy-done
  54.0 17.6 %shard_map.65 = bf16[128,2,32,128]{3,2,1,0:T(8,128)(2,1)} custom-call(f32[8,128]{1,0:T(8,128)} %constant.5.clone.const_ref, f32[128,128]{1,0:T(8,128)} %bitcast.44, bf16[256,256]{1,0:T(8,128)(2,1)} %constant.4.clone.split_ref, bf16[2,2,256,256]{3,2,1,0:T(8,128)(2,1)} %pad_maximum_fusion.3.matrix_x, bf16[2,2,256,256]{3,2,1,0:T(8,128)(2,1)} %pad_maximum_fusion.5.matrix_y, ...), custom_call_target="tpu_custom_call" | custom-call | flops 7000000000 | bytes 4194304 | tf_op jit(solution)/shard_map/pallas_call | solution.py:179
  71.5 10.7 %all-to-all-done.1.refs_0_.refs_1_ = bf16[128,64,128]{2,1,0:T(8,128)(2,1)} async-done(((bf16[128,64,128]{2,1,0:T(8,128)(2,1)}), bf16[128,64,128]{2,1,0:T(8,128)(2,1)}, u32[]{:S(2)}, u32[]{:S(2)}) %all-to-all-start.1) | async-done | bytes 2097184 | tf_op jit(solution)/shard_map/all_to_all | solution.py:244
  82.2 5.6 %all-to-all-start.3 = ((bf16[128,2,32,128]{3,2,1,0:T(8,128)(2,1)}), bf16[128,2,32,128]{3,2,1,0:T(8,128)(2,1)S(1)}, u32[]{:S(2)}, u32[]{:S(2)}) async-start(bf16[128,2,32,128]{3,2,1,0:T(8,128)(2,1)} %shard_map.65), calls=%async_computation.3 | async-start | bytes 4194304 | tf_op jit(solution)/shard_map/all_to_all | solution.py:244
  87.9 17.6 %shard_map.64 = bf16[128,2,32,128]{3,2,1,0:T(8,128)(2,1)} custom-call(f32[8,128]{1,0:T(8,128)} %constant.5.clone.const_ref, f32[128,128]{1,0:T(8,128)} %bitcast.45, bf16[256,256]{1,0:T(8,128)(2,1)} %constant.4.clone.split_ref, bf16[2,2,256,256]{3,2,1,0:T(8,128)(2,1)} %pad_maximum_fusion.3.matrix_x, bf16[2,2,256,256]{3,2,1,0:T(8,128)(2,1)} %pad_maximum_fusion.5.matrix_y, ...), custom_call_target="tpu_custom_call" | custom-call | flops 7000000000 | bytes 4194304 | tf_op jit(solution)/shard_map/pallas_call | solution.py:179
  105.5 11.7 %all-to-all-done.3.in_ref = bf16[128,2,32,128]{3,2,1,0:T(8,128)(2,1)S(1)} async-done(((bf16[128,2,32,128]{3,2,1,0:T(8,128)(2,1)}), bf16[128,2,32,128]{3,2,1,0:T(8,128)(2,1)S(1)}, u32[]{:S(2)}, u32[]{:S(2)}) %all-to-all-start.3) | async-done | bytes 2097184 | tf_op jit(solution)/shard_map/all_to_all | solution.py:244
  117.1 6.1 %all-to-all-start.2 = ((bf16[128,2,32,128]{3,2,1,0:T(8,128)(2,1)}), bf16[128,2,32,128]{3,2,1,0:T(8,128)(2,1)}, u32[]{:S(2)}, u32[]{:S(2)}) async-start(bf16[128,2,32,128]{3,2,1,0:T(8,128)(2,1)} %shard_map.64), calls=%async_computation.2 | async-start | bytes 4194304 | tf_op jit(solution)/shard_map/all_to_all | solution.py:244
  123.2 2.4 %shard_map.66.refs_0_ = f32[128,2,64,128]{3,2,1,0:T(8,128)} custom-call(bf16[128,2,32,128]{3,2,1,0:T(8,128)(2,1)S(1)} %all-to-all-done.3.in_ref), custom_call_target="tpu_custom_call" | custom-call | flops 10000000 | bytes 6291456 | tf_op jit(solution)/shard_map/pallas_call | solution.py:212
  125.7 26.5 %all-to-all-done.2.in_ref = bf16[128,2,32,128]{3,2,1,0:T(8,128)(2,1)} async-done(((bf16[128,2,32,128]{3,2,1,0:T(8,128)(2,1)}), bf16[128,2,32,128]{3,2,1,0:T(8,128)(2,1)}, u32[]{:S(2)}, u32[]{:S(2)}) %all-to-all-start.2) | async-done | bytes 2097184 | tf_op jit(solution)/shard_map/all_to_all | solution.py:244
  152.2 3.6 %shard_map.67 = f32[128,2,64,128]{3,2,1,0:T(8,128)} custom-call(bf16[128,2,32,128]{3,2,1,0:T(8,128)(2,1)} %all-to-all-done.2.in_ref, f32[128,2,64,128]{3,2,1,0:T(8,128)} %shard_map.66.refs_0_), custom_call_target="tpu_custom_call", output_to_operand_aliasing={{}: (1, {})} | custom-call | flops 10000000 | bytes 6291456 | tf_op jit(solution)/shard_map/pallas_call | solution.py:212
  (7 shorter events, 0.2 us)
Async XLA Ops:
  0.0 1.9 %copy-start.3 = (bf16[128,128]{1,0:T(8,128)(2,1)S(1)}, bf16[128,128]{1,0:T(8,128)(2,1)}, u32[]{:S(2)}) copy-start(bf16[128,128]{1,0:T(8,128)(2,1)} %param.7) | copy-start | bytes 98308
  3.6 11.5 %copy-start.2 = (bf16[2,2,2,2,64,64]{5,4,3,2,1,0:T(8,128)(2,1)S(1)}, bf16[2,2,2,2,64,64]{5,4,3,2,1,0:T(8,128)(2,1)}, u32[]{:S(2)}) copy-start(bf16[2,2,2,2,64,64]{5,4,3,2,1,0:T(8,128)(2,1)} %param.8) | copy-start | bytes 393220
  3.6 43.6 %all-to-all-start = ((bf16[128,72,128]{2,1,0:T(8,128)(2,1)}), bf16[128,72,128]{2,1,0:T(8,128)(2,1)S(1)}, u32[]{:S(2)}, u32[]{:S(2)}) async-start(bf16[128,72,128]{2,1,0:T(8,128)(2,1)} %pad_maximum_fusion), calls=%async_computation | async-start | bytes 4718592 | tf_op jit(solution)/shard_map/all_to_all | solution.py:244
  20.3 5.8 %copy-start.1 = (bf16[2,2,64,2,2,64]{5,2,1,4,3,0:T(8,128)(2,1)S(1)}, bf16[2,2,64,2,2,64]{5,2,1,4,3,0:T(8,128)(2,1)}, u32[]{:S(2)}) copy-start(bf16[2,2,64,2,2,64]{5,2,1,4,3,0:T(8,128)(2,1)} %rev.12) | copy-start | bytes 393220
  47.2 6.7 %copy-start = (bf16[128,72,128]{2,1,0:T(8,128)(2,1)}, bf16[128,72,128]{2,1,0:T(8,128)(2,1)S(1)}, u32[]{:S(2)}) copy-start(bf16[128,72,128]{2,1,0:T(8,128)(2,1)S(1)} %all-to-all-done.refs_0_.refs_1_) | copy-start | bytes 7077892
  47.2 35.0 %all-to-all-start.1 = ((bf16[128,64,128]{2,1,0:T(8,128)(2,1)}), bf16[128,64,128]{2,1,0:T(8,128)(2,1)}, u32[]{:S(2)}, u32[]{:S(2)}) async-start(bf16[128,64,128]{2,1,0:T(8,128)(2,1)} %pad_maximum_fusion.1), calls=%async_computation.1 | async-start | bytes 4194304 | tf_op jit(solution)/shard_map/all_to_all | solution.py:244
  82.2 34.9 %all-to-all-start.3 = ((bf16[128,2,32,128]{3,2,1,0:T(8,128)(2,1)}), bf16[128,2,32,128]{3,2,1,0:T(8,128)(2,1)S(1)}, u32[]{:S(2)}, u32[]{:S(2)}) async-start(bf16[128,2,32,128]{3,2,1,0:T(8,128)(2,1)} %shard_map.65), calls=%async_computation.3 | async-start | bytes 4194304 | tf_op jit(solution)/shard_map/all_to_all | solution.py:244
  117.1 35.0 %all-to-all-start.2 = ((bf16[128,2,32,128]{3,2,1,0:T(8,128)(2,1)}), bf16[128,2,32,128]{3,2,1,0:T(8,128)(2,1)}, u32[]{:S(2)}, u32[]{:S(2)}) async-start(bf16[128,2,32,128]{3,2,1,0:T(8,128)(2,1)} %shard_map.64), calls=%async_computation.2 | async-start | bytes 4194304 | tf_op jit(solution)/shard_map/all_to_all | solution.py:244

commit v4 on v3

--- a/solution.py
+++ b/solution.py
@@ -251,8 +251,8 @@
     rows = 2 * size
     split = split_matrix()
     matrices = [pair_matrices(translation[dim]) for dim in range(2)]
-    extra = jnp.broadcast_to(velocity[:, None], (boxes, 8, 128))
-    first = jnp.concatenate([weights[:, :size], weights[:, 64 : 64 + size], extra], 1)
+    first = jnp.concatenate([weights[:, :size], weights[:, 64 : 64 + size + 8]], 1)
+    first = jnp.where(lax.broadcasted_iota(jnp.int32, first.shape, 1) < rows, first, velocity[:, None])
     first, weights = lax.optimization_barrier((first, weights))
     arrived = [exchange(first)]
     second = jnp.concatenate([weights[:, size:64], weights[:, 64 + size :]], 1)

time: 157 us -> 157 us (level)
    select_n x0 -> x1, other arithmetic: none -> 2.11 us  [shards(): jnp.where(lax.broadcasted_iota(jnp.int32, first.shape, 1) < rows, first,...]
    concatenate x1 -> x0, other arithmetic: 1.64 us -> none  [shards(): jnp.concatenate([weights[:, :size], weights[:, 64:64 + size], extra], 1)]
where the time goes in v4:
time: 157 us; the launch traced here: 156 us
  waiting for transfers between devices  58.1 us (37%)
  Pallas kernels  41.2 us (26%)
  starting transfers between devices  29.3 us (19%)
  local copies, waits for them, and re-layouts  16.3 us (10%)
  other arithmetic  10.8 us (7%)
    all_to_all x4, waiting for transfers between devices, exchange(): return lax.all_to_all(values, EVERY, 0, 0, tiled=True)  58.1 us
    pallas_call x2, Pallas kernels, butterfly(): pl.pallas_call(functools.partial(butterfly_kernel, bits=bits, wide=wide,...  35.1 us
    all_to_all x4, starting transfers between devices, exchange(): return lax.all_to_all(values, EVERY, 0, 0, tiled=True)  29.3 us
    pallas_call x2, Pallas kernels, finish(): pl.pallas_call(finish_kernel, grid=(boxes // group,), in_specs=[pl.BlockS...  6.02 us
    another operation x4, other arithmetic, pair_matrices(): rows = jnp.stack([blocks, blocks[:, ::-1]])  3.7 us
    another operation x6, local copies, waits for them, and re-layouts, pair_matrices(): rows = jnp.stack([blocks, blocks[:, ::-1]])  3.47 us
  transfers between devices with their start and end apart: 4, of which 4 were waited for; matrix products, arithmetic and copies ran while one was open for 15% of the time, Pallas kernels for 24%

profile of v4, /device:TPU:1, one launch (start us, length us, event | category | flops | bytes accessed | tf_op | source)
XLA Modules:
  0.0 155.9 jit_solution(736167542588507568)
XLA Ops:
  0.0 0.0 slice-start
  0.0 0.0 slice-start.1
  0.0 0.0 copy-start.3
  0.0 1.2 slice-done
  1.2 0.4 slice-done.1
  1.6 0.0 copy-done.3
  1.7 2.1 %maximum_select_fusion = bf16[128,72,128]{2,1,0:T(8,128)(2,1)} fusion(bf16[128,40,128]{2,1,0:T(8,128)(2,1)S(1)} %slice-done.1, bf16[128,32,128]{2,1,0:T(8,128)(2,1)S(1)} %slice-done, pred[72]{0:T(512)(128)(4,1)S(1)} %iota_compare_fusion, bf16[128,128]{1,0:T(8,128)(2,1)S(1)} %copy-done.3), kind=kLoop, calls=%fused_computation | loop fusion | flops 5898240 | bytes 4751432 | tf_op jit(solution)/shard_map/jit(_where)/select_n | solution.py:255
  3.8 0.0 copy-start.2
  3.8 11.5 %all-to-all-start = ((bf16[128,72,128]{2,1,0:T(8,128)(2,1)}), bf16[128,72,128]{2,1,0:T(8,128)(2,1)S(1)}, u32[]{:S(2)}, u32[]{:S(2)}) async-start(bf16[128,72,128]{2,1,0:T(8,128)(2,1)} %maximum_select_fusion), calls=%async_computation | async-start | bytes 4718592 | tf_op jit(solution)/shard_map/all_to_all | solution.py:244
  15.3 0.0 copy-done.2
  15.4 0.1 maximum_bitcast_fusion
  15.4 0.8 fusion.2
  16.2 0.7 rev.12
  16.9 1.0 copy.9
  17.9 0.1 maximum_bitcast_fusion.2
  17.9 0.7 fusion
  18.7 0.7 rev.14
  19.4 1.0 copy.13
  20.4 0.0 copy-start.1
  20.4 1.1 pad_maximum_fusion.1
  21.5 0.8 rev.13
  22.3 1.6 %copy.11 = bf16[2,2,2,64,2,2,64]{6,5,4,3,2,1,0:T(2,128)(2,1)S(1)} copy(bf16[2,2,2,64,2,2,64]{6,3,2,5,4,1,0:T(8,128)(2,1)} %rev.13) | data formatting | bytes 524288 | tf_op jit(solution)/shard_map/rev | solution.py:230
  23.9 1.0 stack.87
  25.0 1.2 stack.81
  26.2 0.0 copy-done.1
  26.2 0.3 copy.10
  26.4 0.9 stack.82
  27.3 1.1 pad_maximum_fusion.3
  28.5 0.5 copy.15
  29.0 0.3 stack.100
  29.3 1.2 stack.94
  30.5 1.2 copy.14
  31.8 0.2 stack.95
  32.0 1.8 %pad_maximum_fusion.2.matrix_x = bf16[2,2,256,256]{3,2,1,0:T(8,128)(2,1)} fusion(bf16[2,1,256,256]{3,2,1,0:T(8,128)(2,1)} %stack.87, bf16[1,1,256,256]{3,2,1,0:T(8,128)(2,1)} %stack.82, bf16[1,1,256,256]{3,2,1,0:T(8,128)(2,1)S(1)} %stack.81), kind=kLoop, calls=%fused_computation.3 | loop fusion | flops 524288 | bytes 1048576 | tf_op jit(solution)/shard_map/stack | solution.py:230
  33.8 0.8 pad_maximum_fusion.4.matrix_y
  34.7 1.9 %fusion.6 = (bf16[128,32,128]{2,1,0:T(8,128)(2,1)S(1)}, bf16[128,32,128]{2,1,0:T(8,128)(2,1)S(1)}) fusion(bf16[128,128,128]{2,1,0:T(8,128)(2,1)} %param.6), kind=kLoop, calls=%fused_computation.28 | loop fusion | bytes 4194304 | tf_op jit(solution)/shard_map/slice | solution.py:258
  36.6 1.6 pad_maximum_fusion
  38.1 9.2 %all-to-all-done.refs_0_.refs_1_ = bf16[128,72,128]{2,1,0:T(8,128)(2,1)S(1)} async-done(((bf16[128,72,128]{2,1,0:T(8,128)(2,1)}), bf16[128,72,128]{2,1,0:T(8,128)(2,1)S(1)}, u32[]{:S(2)}, u32[]{:S(2)}) %all-to-all-start) | async-done | bytes 2359328 | tf_op jit(solution)/shard_map/all_to_all | solution.py:244
  47.4 0.0 copy-start
  47.4 6.1 %all-to-all-start.1 = ((bf16[128,64,128]{2,1,0:T(8,128)(2,1)}), bf16[128,64,128]{2,1,0:T(8,128)(2,1)}, u32[]{:S(2)}, u32[]{:S(2)}) async-start(bf16[128,64,128]{2,1,0:T(8,128)(2,1)} %pad_maximum_fusion), calls=%async_computation.1 | async-start | bytes 4194304 | tf_op jit(solution)/shard_map/all_to_all | solution.py:244
  53.4 0.7 slice_convert_fusion
  54.1 0.0 copy-done
  54.1 17.5 %shard_map.65 = bf16[128,2,32,128]{3,2,1,0:T(8,128)(2,1)} custom-call(f32[8,128]{1,0:T(8,128)} %constant.7.clone.const_ref, f32[128,128]{1,0:T(8,128)} %bitcast.44, bf16[256,256]{1,0:T(8,128)(2,1)} %constant.6.clone.split_ref, bf16[2,2,256,256]{3,2,1,0:T(8,128)(2,1)} %pad_maximum_fusion.2.matrix_x, bf16[2,2,256,256]{3,2,1,0:T(8,128)(2,1)} %pad_maximum_fusion.4.matrix_y, ...), custom_call_target="tpu_custom_call" | custom-call | flops 7000000000 | bytes 4194304 | tf_op jit(solution)/shard_map/pallas_call | solution.py:179
  71.6 10.7 %all-to-all-done.1.refs_0_.refs_1_ = bf16[128,64,128]{2,1,0:T(8,128)(2,1)} async-done(((bf16[128,64,128]{2,1,0:T(8,128)(2,1)}), bf16[128,64,128]{2,1,0:T(8,128)(2,1)}, u32[]{:S(2)}, u32[]{:S(2)}) %all-to-all-start.1) | async-done | bytes 2097184 | tf_op jit(solution)/shard_map/all_to_all | solution.py:244
  82.4 5.6 %all-to-all-start.3 = ((bf16[128,2,32,128]{3,2,1,0:T(8,128)(2,1)}), bf16[128,2,32,128]{3,2,1,0:T(8,128)(2,1)S(1)}, u32[]{:S(2)}, u32[]{:S(2)}) async-start(bf16[128,2,32,128]{3,2,1,0:T(8,128)(2,1)} %shard_map.65), calls=%async_computation.3 | async-start | bytes 4194304 | tf_op jit(solution)/shard_map/all_to_all | solution.py:244
  88.0 17.6 %shard_map.64 = bf16[128,2,32,128]{3,2,1,0:T(8,128)(2,1)} custom-call(f32[8,128]{1,0:T(8,128)} %constant.7.clone.const_ref, f32[128,128]{1,0:T(8,128)} %bitcast.45, bf16[256,256]{1,0:T(8,128)(2,1)} %constant.6.clone.split_ref, bf16[2,2,256,256]{3,2,1,0:T(8,128)(2,1)} %pad_maximum_fusion.2.matrix_x, bf16[2,2,256,256]{3,2,1,0:T(8,128)(2,1)} %pad_maximum_fusion.4.matrix_y, ...), custom_call_target="tpu_custom_call" | custom-call | flops 7000000000 | bytes 4194304 | tf_op jit(solution)/shard_map/pallas_call | solution.py:179
  105.6 11.7 %all-to-all-done.3.in_ref = bf16[128,2,32,128]{3,2,1,0:T(8,128)(2,1)S(1)} async-done(((bf16[128,2,32,128]{3,2,1,0:T(8,128)(2,1)}), bf16[128,2,32,128]{3,2,1,0:T(8,128)(2,1)S(1)}, u32[]{:S(2)}, u32[]{:S(2)}) %all-to-all-start.3) | async-done | bytes 2097184 | tf_op jit(solution)/shard_map/all_to_all | solution.py:244
  117.3 6.1 %all-to-all-start.2 = ((bf16[128,2,32,128]{3,2,1,0:T(8,128)(2,1)}), bf16[128,2,32,128]{3,2,1,0:T(8,128)(2,1)}, u32[]{:S(2)}, u32[]{:S(2)}) async-start(bf16[128,2,32,128]{3,2,1,0:T(8,128)(2,1)} %shard_map.64), calls=%async_computation.2 | async-start | bytes 4194304 | tf_op jit(solution)/shard_map/all_to_all | solution.py:244
  123.4 2.4 %shard_map.66.refs_0_ = f32[128,2,64,128]{3,2,1,0:T(8,128)} custom-call(bf16[128,2,32,128]{3,2,1,0:T(8,128)(2,1)S(1)} %all-to-all-done.3.in_ref), custom_call_target="tpu_custom_call" | custom-call | flops 10000000 | bytes 6291456 | tf_op jit(solution)/shard_map/pallas_call | solution.py:212
  125.8 26.5 %all-to-all-done.2.in_ref = bf16[128,2,32,128]{3,2,1,0:T(8,128)(2,1)} async-done(((bf16[128,2,32,128]{3,2,1,0:T(8,128)(2,1)}), bf16[128,2,32,128]{3,2,1,0:T(8,128)(2,1)}, u32[]{:S(2)}, u32[]{:S(2)}) %all-to-all-start.2) | async-done | bytes 2097184 | tf_op jit(solution)/shard_map/all_to_all | solution.py:244
  152.3 3.6 %shard_map.67 = f32[128,2,64,128]{3,2,1,0:T(8,128)} custom-call(bf16[128,2,32,128]{3,2,1,0:T(8,128)(2,1)} %all-to-all-done.2.in_ref, f32[128,2,64,128]{3,2,1,0:T(8,128)} %shard_map.66.refs_0_), custom_call_target="tpu_custom_call", output_to_operand_aliasing={{}: (1, {})} | custom-call | flops 10000000 | bytes 6291456 | tf_op jit(solution)/shard_map/pallas_call | solution.py:212
  (7 shorter events, 0.1 us)
Async XLA Ops:
  0.0 1.2 slice-start
  0.0 1.6 %slice-start.1 = ((bf16[128,128,128]{2,1,0:T(8,128)(2,1)}), bf16[128,40,128]{2,1,0:T(8,128)(2,1)S(1)}, s32[]{:S(2)}) async-start(bf16[128,128,128]{2,1,0:T(8,128)(2,1)} %param.6), calls=%async_computation.5 | async-start | bytes 2621440 | tf_op jit(solution)/shard_map/slice | solution.py:254
  0.0 1.6 %copy-start.3 = (bf16[128,128]{1,0:T(8,128)(2,1)S(1)}, bf16[128,128]{1,0:T(8,128)(2,1)}, u32[]{:S(2)}) copy-start(bf16[128,128]{1,0:T(8,128)(2,1)} %param.7) | copy-start | bytes 98308
  3.8 11.5 %copy-start.2 = (bf16[2,2,2,2,64,64]{5,4,3,2,1,0:T(8,128)(2,1)S(1)}, bf16[2,2,2,2,64,64]{5,4,3,2,1,0:T(8,128)(2,1)}, u32[]{:S(2)}) copy-start(bf16[2,2,2,2,64,64]{5,4,3,2,1,0:T(8,128)(2,1)} %param.8) | copy-start | bytes 393220
  3.8 43.6 %all-to-all-start = ((bf16[128,72,128]{2,1,0:T(8,128)(2,1)}), bf16[128,72,128]{2,1,0:T(8,128)(2,1)S(1)}, u32[]{:S(2)}, u32[]{:S(2)}) async-start(bf16[128,72,128]{2,1,0:T(8,128)(2,1)} %maximum_select_fusion), calls=%async_computation | async-start | bytes 4718592 | tf_op jit(solution)/shard_map/all_to_all | solution.py:244
  20.4 5.8 %copy-start.1 = (bf16[2,2,64,2,2,64]{5,2,1,4,3,0:T(8,128)(2,1)S(1)}, bf16[2,2,64,2,2,64]{5,2,1,4,3,0:T(8,128)(2,1)}, u32[]{:S(2)}) copy-start(bf16[2,2,64,2,2,64]{5,2,1,4,3,0:T(8,128)(2,1)} %rev.12) | copy-start | bytes 393220
  47.4 6.7 %copy-start = (bf16[128,72,128]{2,1,0:T(8,128)(2,1)}, bf16[128,72,128]{2,1,0:T(8,128)(2,1)S(1)}, u32[]{:S(2)}) copy-start(bf16[128,72,128]{2,1,0:T(8,128)(2,1)S(1)} %all-to-all-done.refs_0_.refs_1_) | copy-start | bytes 7077892
  47.4 35.0 %all-to-all-start.1 = ((bf16[128,64,128]{2,1,0:T(8,128)(2,1)}), bf16[128,64,128]{2,1,0:T(8,128)(2,1)}, u32[]{:S(2)}, u32[]{:S(2)}) async-start(bf16[128,64,128]{2,1,0:T(8,128)(2,1)} %pad_maximum_fusion), calls=%async_computation.1 | async-start | bytes 4194304 | tf_op jit(solution)/shard_map/all_to_all | solution.py:244
  82.4 34.9 %all-to-all-start.3 = ((bf16[128,2,32,128]{3,2,1,0:T(8,128)(2,1)}), bf16[128,2,32,128]{3,2,1,0:T(8,128)(2,1)S(1)}, u32[]{:S(2)}, u32[]{:S(2)}) async-start(bf16[128,2,32,128]{3,2,1,0:T(8,128)(2,1)} %shard_map.65), calls=%async_computation.3 | async-start | bytes 4194304 | tf_op jit(solution)/shard_map/all_to_all | solution.py:244
  117.3 35.0 %all-to-all-start.2 = ((bf16[128,2,32,128]{3,2,1,0:T(8,128)(2,1)}), bf16[128,2,32,128]{3,2,1,0:T(8,128)(2,1)}, u32[]{:S(2)}, u32[]{:S(2)}) async-start(bf16[128,2,32,128]{3,2,1,0:T(8,128)(2,1)} %shard_map.64), calls=%async_computation.2 | async-start | bytes 4194304 | tf_op jit(solution)/shard_map/all_to_all | solution.py:244
